TPU v7x, 32 devices: a whole 2x2x4 slice. The times are simulated.
32 devices in a mesh: lat: 4 (over z), lon: 4 (over x, core), ens: 2 (over y).
Axes of the slice: x: 2, y: 2, z: 4, core: 2. Of those that a mesh axis runs over, the one named last changes fastest.
Arguments:
- initial_state: bfloat16 [2, 128, 256, 256], P('ens', 'lat', 'lon'), may hold values from -6 to 6
- background: bfloat16 [2, 128, 256, 256], P('ens', 'lat', 'lon'), may hold values from -6 to 6
- background_precision: float32 [256], replicated, may hold values from 0.5 to 4
- kernel_taps: float32 [2, 25, 256], replicated, may hold values from -1 to 1
- norm_gains: float32 [2, 256], replicated, may hold values from 0.5 to 2
- weight_in: bfloat16 [2, 256, 512], replicated, may hold values from -0.375 to 0.375
- weight_out: bfloat16 [2, 512, 256], replicated, may hold values from -0.25 to 0.25
- obs_operator: bfloat16 [256, 128], replicated, may hold values from -0.375 to 0.375
- obs_precision: float32 [128], replicated, may hold values from 0.5 to 4
- obs_values: bfloat16 [8192, 128], P(('lat', 'lon')), may hold values from -6 to 6
- obs_owner: int32 [8192, 1], P(('lat', 'lon')), may hold values from 0 to 15; in each aligned block of 512 rows (0 to 511, 512 to 1023, ...) at most 64 rows name the same one
- obs_cell: int32 [8192], P(('lat', 'lon')), may hold values from 0 to 2047
Outputs:
- gradient: float32 [2, 128, 256, 256], P('ens', 'lat', 'lon')
Inputs may be any that keep to these rules, and one draw needn't show every extreme that they name: `obs_owner`: among the 512 footprints of one device, no owner is named more than 64 times; in every draw some device names one owner exactly 64 times. Owner numbers run over the lat index times the lon axis's device count plus the lon index. `obs_cell`: cells are numbered row by row over the owner's 32 x 64 block.
All inputs are finite; a program needn't handle non-finite values.
Results may differ from a plain program's by a relative error of at most 0.006.
Values may be sent and summed in bfloat16 or wider, within the bound.
A program may use at most 128 MiB of HBM per device.

v0:
```python
import jax
import jax.numpy as jnp
from jax import lax
from jax.sharding import PartitionSpec as P

SQRT_TWO_OVER_PI = 0.7978845608
CUBIC = 0.044715
EPSILON = 1e-06


def extended(block, sides, width):
    for axis, dim in sides:
        count = lax.axis_size(axis)
        forward = [(i, i + 1) for i in range(count - 1)]
        forward.append((count - 1, 0))
        backward = [(target, source) for source, target in forward]
        low = lax.ppermute(
            lax.slice_in_dim(block, block.shape[dim] - width, None, axis=dim), axis, forward
        )
        high = lax.ppermute(lax.slice_in_dim(block, 0, width, axis=dim), axis, backward)
        block = jnp.concatenate([low, block, high], axis=dim)
    return block


def gelu_value(values):
    return (
        0.5
        * values
        * (1.0 + jnp.tanh(SQRT_TWO_OVER_PI * (values + CUBIC * values * values * values)))
    )


def gelu_slope(values):
    inner = jnp.tanh(SQRT_TWO_OVER_PI * (values + CUBIC * values * values * values))
    return 0.5 * (1.0 + inner) + 0.5 * values * (1.0 - inner * inner) * SQRT_TWO_OVER_PI * (
        1.0 + 3.0 * CUBIC * values * values
    )


def polar(padded, depth):
    lat_band = lax.axis_index("lat")
    last_band = lax.axis_size("lat") - 1
    row_index = jnp.arange(padded.shape[0], dtype=jnp.int32)[:, None, None]
    outside = (row_index < depth) & (lat_band == 0) | (row_index >= padded.shape[0] - depth) & (
        lat_band == last_band
    )
    return jnp.where(outside, jnp.zeros_like(padded), padded)


def state_rim(field):
    return polar(extended(field, (("lat", 0), ("lon", 1)), 2), 2)


def cotangent_rim(field):
    return polar(extended(field, (("lat", 0), ("lon", 1)), 2), 2)


def depthwise(padded, kernel, height, width):
    summed = jnp.zeros((height, width, padded.shape[2]), jnp.float32)
    for row_tap in range(5):
        for col_tap in range(5):
            summed = summed + kernel[5 * row_tap + col_tap] * padded[
                row_tap : row_tap + height, col_tap : col_tap + width
            ].astype(jnp.float32)
    return summed


def transposed(padded, kernel, height, width):
    summed = jnp.zeros((height, width, padded.shape[2]), jnp.float32)
    for row_tap in range(5):
        for col_tap in range(5):
            summed = summed + kernel[5 * row_tap + col_tap] * padded[
                4 - row_tap : 4 - row_tap + height, 4 - col_tap : 4 - col_tap + width
            ].astype(jnp.float32)
    return summed


def layer_front(conv_out, gain_row, layer_in, layer_out):
    channels = conv_out.shape[-1]
    flat_conv = conv_out.reshape(-1, channels)
    inverse_rms = lax.rsqrt(jnp.mean(flat_conv * flat_conv, axis=1, keepdims=True) + EPSILON)
    normed = (flat_conv * inverse_rms * gain_row).astype(jnp.bfloat16)
    hidden = jnp.dot(normed, layer_in, preferred_element_type=jnp.float32)
    active = gelu_value(hidden).astype(jnp.bfloat16)
    mixed = jnp.dot(active, layer_out, preferred_element_type=jnp.float32)
    return (mixed.reshape(conv_out.shape), hidden)


def layer_back(conv_out, hidden, upstream, gain_row, layer_in, layer_out):
    channels = conv_out.shape[-1]
    flat_conv = conv_out.reshape(-1, channels)
    inverse_rms = lax.rsqrt(jnp.mean(flat_conv * flat_conv, axis=1, keepdims=True) + EPSILON)
    back_hidden = jnp.dot(
        upstream.reshape(-1, channels).astype(jnp.bfloat16),
        layer_out.T,
        preferred_element_type=jnp.float32,
    )
    hidden_grad = (back_hidden * gelu_slope(hidden)).astype(jnp.bfloat16)
    normed_grad = jnp.dot(hidden_grad, layer_in.T, preferred_element_type=jnp.float32)
    weighted = normed_grad * gain_row
    cube = inverse_rms * inverse_rms * inverse_rms
    conv_grad = inverse_rms * weighted - flat_conv * cube * jnp.mean(
        weighted * flat_conv, axis=1, keepdims=True
    )
    return conv_grad.astype(jnp.bfloat16).reshape(conv_out.shape)


def per_device(
    initial_state,
    background,
    background_precision,
    kernel_taps,
    norm_gains,
    weight_in,
    weight_out,
    obs_operator,
    obs_precision,
    obs_values,
    obs_owner,
    obs_cell,
):
    start_state = initial_state[0]
    height, width, channels = start_state.shape
    first_conv = depthwise(state_rim(start_state), kernel_taps[0], height, width)
    first_mix, first_hidden = layer_front(first_conv, norm_gains[0], weight_in[0], weight_out[0])
    middle = (start_state.astype(jnp.float32) + first_mix).astype(jnp.bfloat16)
    second_conv = depthwise(state_rim(middle), kernel_taps[1], height, width)
    second_mix, second_hidden = layer_front(second_conv, norm_gains[1], weight_in[1], weight_out[1])
    final_state = (middle.astype(jnp.float32) + second_mix).astype(jnp.bfloat16)
    lat_count = lax.axis_size("lat")
    lon_count = lax.axis_size("lon")
    grid_count = lat_count * lon_count
    footprint_count = obs_values.shape[0]
    obs_channels = obs_values.shape[1]
    capacity = 2 * footprint_count // grid_count
    owner_ids = obs_owner[:, 0]
    owner_hits = (owner_ids[:, None] == jnp.arange(grid_count, dtype=jnp.int32)[None, :]).astype(
        jnp.int32
    )
    earlier = jnp.cumsum(owner_hits, axis=0) - owner_hits
    rank_slot = jnp.sum(earlier * owner_hits, axis=1)
    slot_index = owner_ids * capacity + rank_slot
    send_values = (
        jnp.zeros((grid_count * capacity, obs_channels), jnp.bfloat16)
        .at[slot_index]
        .set(obs_values)
    )
    send_cells = jnp.full((grid_count * capacity,), -1, jnp.int32).at[slot_index].set(obs_cell)
    recv_values, recv_cells = (
        lax.all_to_all(
            send_values.reshape(grid_count, capacity, obs_channels),
            ("lat", "lon"),
            split_axis=0,
            concat_axis=0,
            tiled=True,
        ),
        lax.all_to_all(
            send_cells.reshape(grid_count, capacity),
            ("lat", "lon"),
            split_axis=0,
            concat_axis=0,
            tiled=True,
        ),
    )
    flat_values = recv_values.reshape(grid_count * capacity, obs_channels)
    flat_cells = recv_cells.reshape(grid_count * capacity)
    occupied = flat_cells >= 0
    cell_safe = jnp.maximum(flat_cells, 0)
    state_rows = jnp.take(final_state.reshape(height * width, channels), cell_safe, axis=0)
    predicted = jnp.where(
        occupied[:, None],
        jnp.dot(state_rows, obs_operator, preferred_element_type=jnp.float32),
        0.0,
    )
    ensemble_sum = lax.psum(predicted, "ens")
    members = lax.axis_size("ens")
    mean_pred = ensemble_sum / members
    misfit = obs_precision * (mean_pred - flat_values.astype(jnp.float32)) / members
    obs_adjoint = jnp.where(occupied[:, None], misfit, 0.0).astype(jnp.bfloat16)
    spread = jnp.dot(obs_adjoint, obs_operator.T, preferred_element_type=jnp.float32)
    upstream = (
        jnp.zeros((height * width, channels), jnp.float32)
        .at[cell_safe]
        .add(spread)
        .reshape(height, width, channels)
    )
    second_grad = layer_back(
        second_conv, second_hidden, upstream, norm_gains[1], weight_in[1], weight_out[1]
    )
    upstream = upstream + transposed(cotangent_rim(second_grad), kernel_taps[1], height, width)
    first_grad = layer_back(
        first_conv, first_hidden, upstream, norm_gains[0], weight_in[0], weight_out[0]
    )
    upstream = upstream + transposed(cotangent_rim(first_grad), kernel_taps[0], height, width)
    prior = background_precision * (
        start_state.astype(jnp.float32) - background[0].astype(jnp.float32)
    )
    return (prior + upstream)[None]


def solution(mesh):
    in_specs = (
        P("ens", "lat", "lon", None),
        P("ens", "lat", "lon", None),
        P(),
        P(),
        P(),
        P(),
        P(),
        P(),
        P(),
        P(("lat", "lon"), None),
        P(("lat", "lon"), None),
        P(("lat", "lon")),
    )
    out_specs = P("ens", "lat", "lon", None)
    return jax.shard_map(
        per_device, mesh=mesh, in_specs=in_specs, out_specs=out_specs, check_vma=False
    )
```

profile of v0, /device:TPU:0, one launch (start us, length us, event | category | flops | bytes accessed | tf_op | source)
XLA Modules:
  0.0 189.5 jit_solution(3692091830096950959)
XLA Ops:
  6.5 1.0 slice_bitcast_fusion.1
  7.5 3.1 %collective-permute-start = (bf16[2,64,256]{2,1,0:T(8,128)(2,1)S(1)}, bf16[2,64,256]{2,1,0:T(8,128)(2,1)S(1)}, u32[]{:S(2)}, u32[]{:S(2)}) collective-permute-start(bf16[2,64,256]{2,1,0:T(8,128)(2,1)S(1)} %get-tuple-element.27), channel_id=1, source_target_pairs={{0,8},{8,16},{16,24},{24,0},{1,9},{9,17},{17,25},{25,1},{2,10},{10... | collective-permute-start | bytes 196616 | tf_op jit(solution)/shard_map/ppermute | solution.py:17
  10.6 2.1 %collective-permute-start.1 = (bf16[2,64,256]{2,1,0:T(8,128)(2,1)S(1)}, bf16[2,64,256]{2,1,0:T(8,128)(2,1)S(1)}, u32[]{:S(2)}, u32[]{:S(2)}) collective-permute-start(bf16[2,64,256]{2,1,0:T(8,128)(2,1)S(1)} %get-tuple-element.28), channel_id=1, source_target_pairs={{8,0},{16,8},{24,16},{0,24},{9,1},{17,9},{25,17},{1,25},{10,2},{18... | collective-permute-start | bytes 196616 | tf_op jit(solution)/shard_map/ppermute | solution.py:20
  12.7 0.7 fusion.70
  13.4 1.1 reduce-window.6
  14.5 0.2 slice_reduce_fusion
  14.8 0.8 fusion.69
  15.5 0.7 compare_select_fusion
  16.2 2.6 %scatter_custom_fusion = s32[1024]{0:T(1024)S(1)} fusion(s32[512]{0:T(512)S(1)} %bitcast.267, s32[512]{0:T(512)} %param.23, s32[]{:T(128)} %constant.20.clone.1), kind=kCustom, calls=%fused_computation.127 | custom fusion | bytes 4608 | tf_op jit(solution)/shard_map/scatter | solution.py:148
  18.8 0.7 all_to_all.9
  19.5 4.3 %all-to-all-start = ((s32[16,1,64]{2,1,0:T(1,128)}), s32[16,1,64]{2,1,0:T(1,128)S(1)}, u32[]{:S(2)}, u32[]{:S(2)}) async-start(s32[16,1,64]{2,1,0:T(1,128)} %all_to_all.9), calls=%async_computation | async-start | bytes 16384 | tf_op jit(solution)/shard_map/all_to_all | solution.py:157
  23.8 1.5 fusion.91
  25.5 1.5 fusion.92
  26.9 0.9 fusion.90
  28.0 1.4 fusion.93
  29.4 0.6 and_or_fusion
  30.0 1.0 pad_maximum_fusion.11
  31.0 0.5 collective-permute-start.2
  31.5 1.3 collective-permute-start.3
  32.9 1.5 collective-permute-done.2
  34.4 1.1 maximum_select_fusion
  35.6 7.9 %multiply_reduce_fusion.1 = (f32[32,64]{1,0:T(8,128)S(1)}, f32[32,64,256]{2,1,0:T(8,128)S(1)}) fusion(bf16[36,68,256]{2,1,0:T(8,128)(2,1)S(1)} %maximum_select_fusion, f32[256]{0:T(256)S(1)} %bitcast.236, f32[256]{0:T(256)S(1)} %bitcast.238, f32[256]{0:T(256)S(1)} %bitcast.240, f32[256]{0:T(256)S(1)} %bitcast.242, f32[256]{0:T(256)S(1)} %bitcast.244, ...), kind=kLoop, calls=%fused_computation.50 | loop fusion | flops 39843840 | bytes 28345344 | tf_op jit(solution)/shard_map/reduce_sum | solution.py:81
  43.6 1.1 multiply_convert_fusion.3
  44.7 3.4 %multiply_convert_fusion.1 = (bf16[2048,512]{1,0:T(8,128)(2,1)S(1)}, f32[2048,512]{1,0:T(8,128)}) fusion(bf16[2048,256]{1,0:T(8,128)(2,1)S(1)} %bitcast.177, bf16[2,256,512]{2,1,0:T(8,128)(2,1)S(1)} %copy-done.78), kind=kOutput, calls=%fused_computation.23 | convolution fusion | flops 546308096 | bytes 7602176 | tf_op jit(solution)/shard_map/dot_general | solution.py:83
  48.1 0.7 fusion.17
  48.8 2.0 %collective-permute-start.4 = (bf16[2,64,256]{2,1,0:T(8,128)(2,1)S(1)}, bf16[2,64,256]{2,1,0:T(8,128)(2,1)S(1)}, u32[]{:S(2)}, u32[]{:S(2)}) collective-permute-start(bf16[2,64,256]{2,1,0:T(8,128)(2,1)S(1)} %get-tuple-element.25), channel_id=1, source_target_pairs={{0,8},{8,16},{16,24},{24,0},{1,9},{9,17},{17,25},{25,1},{2,10},{10... | collective-permute-start | bytes 196616 | tf_op jit(solution)/shard_map/ppermute | solution.py:17
  50.8 1.9 %collective-permute-start.5 = (bf16[2,64,256]{2,1,0:T(8,128)(2,1)S(1)}, bf16[2,64,256]{2,1,0:T(8,128)(2,1)S(1)}, u32[]{:S(2)}, u32[]{:S(2)}) collective-permute-start(bf16[2,64,256]{2,1,0:T(8,128)(2,1)S(1)} %get-tuple-element.26), channel_id=1, source_target_pairs={{8,0},{16,8},{24,16},{0,24},{9,1},{17,9},{25,17},{1,25},{10,2},{18... | collective-permute-start | bytes 196616 | tf_op jit(solution)/shard_map/ppermute | solution.py:20
  52.7 2.3 %collective-permute-done.4 = bf16[2,64,256]{2,1,0:T(8,128)(2,1)S(1)} collective-permute-done((bf16[2,64,256]{2,1,0:T(8,128)(2,1)S(1)}, bf16[2,64,256]{2,1,0:T(8,128)(2,1)S(1)}, u32[]{:S(2)}, u32[]{:S(2)}) %collective-permute-start.4) | collective-permute-done | bytes 65568 | tf_op jit(solution)/shard_map/ppermute | solution.py:17
  55.0 2.0 %collective-permute-done.5 = bf16[2,64,256]{2,1,0:T(8,128)(2,1)S(1)} collective-permute-done((bf16[2,64,256]{2,1,0:T(8,128)(2,1)S(1)}, bf16[2,64,256]{2,1,0:T(8,128)(2,1)S(1)}, u32[]{:S(2)}, u32[]{:S(2)}) %collective-permute-start.5) | collective-permute-done | bytes 65568 | tf_op jit(solution)/shard_map/ppermute | solution.py:20
  57.3 1.6 collective-permute-start.7
  59.1 1.4 collective-permute-done.6
  60.5 1.7 maximum_select_fusion.1
  62.5 7.0 %multiply_reduce_fusion = (f32[32,64]{1,0:T(8,128)S(1)}, f32[32,64,256]{2,1,0:T(8,128)S(1)}) fusion(bf16[36,68,256]{2,1,0:T(8,128)(2,1)S(1)} %maximum_select_fusion.1, f32[256]{0:T(256)S(1)} %bitcast.196, f32[256]{0:T(256)S(1)} %bitcast.194, f32[256]{0:T(256)S(1)} %bitcast.200, f32[256]{0:T(256)S(1)} %bitcast.202, f32[256]{0:T(256)S(1)} %bitcast.204, ...), kind=kLoop, calls=%fused_computation.47 | loop fusion | flops 39843840 | bytes 28345344 | tf_op jit(solution)/shard_map/reduce_sum | solution.py:81
  69.6 0.4 multiply_convert_fusion.2
  70.0 1.0 copy-done.79
  71.0 3.4 %multiply_convert_fusion = (bf16[2048,512]{1,0:T(8,128)(2,1)S(1)}, f32[2048,512]{1,0:T(8,128)}) fusion(bf16[2048,256]{1,0:T(8,128)(2,1)S(1)} %bitcast.178, bf16[2,256,512]{2,1,0:T(8,128)(2,1)S(1)} %copy-done.79), kind=kOutput, calls=%fused_computation.22 | convolution fusion | flops 546308096 | bytes 7602176 | tf_op jit(solution)/shard_map/dot_general | solution.py:83
  74.4 0.7 add_convert_fusion
  75.1 5.0 %gather_fusion = bf16[1024,256]{1,0:T(8,128)(2,1)} fusion(bf16[2048,256]{1,0:T(8,128)(2,1)S(1)} %bitcast.168, s32[1024]{0:T(1024)S(1)} %broadcast_clamp_fusion), kind=kCustom, calls=%fused_computation | custom fusion | bytes 1052672 | tf_op jit(solution)/shard_map/jit(_take)/gather | solution.py:169
  80.1 2.2 %convolution_select_fusion = f32[1024,128]{1,0:T(8,128)} fusion(bf16[256,128]{1,0:T(8,128)(2,1)S(1)} %copy-done, bf16[1024,256]{1,0:T(8,128)(2,1)} %gather_fusion, pred[1024]{0:T(1024)(128)(4,1)S(1)} %le.16, pred[1024]{0:T(1024)(128)(4,1)S(1)} %ge.29), kind=kOutput, calls=%fused_computation.56 | convolution fusion | flops 67502080 | bytes 1116160 | tf_op jit(solution)/shard_map/dot_general | solution.py:172
  82.4 2.8 %scatter_custom_fusion.1 = bf16[1024,128]{1,0:T(8,128)(2,1)} fusion(s32[512]{0:T(512)S(1)} %bitcast.268, bf16[512,128]{1,0:T(8,128)(2,1)} %param.21, bf16[]{:T(256)} %constant.30.clone.1), kind=kCustom, calls=%fused_computation.91 | custom fusion | bytes 262656 | tf_op jit(solution)/shard_map/scatter | solution.py:146
  85.2 4.8 %all-to-all-start.1 = ((bf16[16,64,128]{2,1,0:T(8,128)(2,1)}), bf16[16,64,128]{2,1,0:T(8,128)(2,1)S(1)}, u32[]{:S(2)}, u32[]{:S(2)}) async-start(bf16[16,64,128]{2,1,0:T(8,128)(2,1)} %bitcast.72), calls=%async_computation.1 | async-start | bytes 524288 | tf_op jit(solution)/shard_map/all_to_all | solution.py:150
  90.0 10.0 %all-to-all-done.1 = bf16[16,64,128]{2,1,0:T(8,128)(2,1)S(1)} async-done(((bf16[16,64,128]{2,1,0:T(8,128)(2,1)}), bf16[16,64,128]{2,1,0:T(8,128)(2,1)S(1)}, u32[]{:S(2)}, u32[]{:S(2)}) %all-to-all-start.1) | async-done | bytes 262176 | tf_op jit(solution)/shard_map/all_to_all | solution.py:150
  100.0 11.3 %all-reduce.2.cloned.1.call-done = f32[1024,128]{1,0:T(8,128)} async-done(((f32[1024,128]{1,0:T(8,128)}), f32[1024,128]{1,0:T(8,128)}) %all-reduce.2.cloned.1.call-update) | async-done | bytes 524304 | tf_op jit(solution)/shard_map/psum | solution.py:175
  111.3 1.4 fusion.36
  112.7 8.2 %scatter_custom_fusion.2 = f32[2048,256]{1,0:T(8,128)} fusion(s32[1024]{0:T(1024)S(1)} %reshape.327, f32[1024,256]{1,0:T(8,128)S(1)} %fusion.36, f32[]{:T(128)} %constant.19.clone.1), kind=kCustom, calls=%fused_computation.58 | custom fusion | flops 262144 | bytes 2097156 | tf_op jit(solution)/shard_map/scatter-add | solution.py:184
  120.9 8.2 %fusion.25 = (f32[2048]{0:T(1024)S(1)}, f32[2048,256]{1,0:T(8,128)}) fusion(f32[32,64,256]{2,1,0:T(8,128)} %copy-done.1, f32[256]{0:T(256)S(1)} %bitcast.266, bf16[2,256,512]{2,1,0:T(8,128)(2,1)} %param.17, f32[2048,512]{1,0:T(8,128)} %get-tuple-element.84, f32[2048,256]{1,0:T(8,128)} %scatter_custom_fusion.2, bf16[2,512,256]{2,1,0:T(8,128)(2,1)} %param.18), kind=kOutput, calls=%fused_computation.43 | convolution fusion | flops 1095759872 | bytes 11019264 | tf_op jit(solution)/shard_map/dot_general | solution.py:99
  129.0 2.7 %fusion.24 = bf16[2048,256]{1,0:T(8,128)(2,1)S(1)} fusion(f32[32,64,256]{2,1,0:T(8,128)} %copy-done.1, f32[2048,256]{1,0:T(8,128)} %get-tuple-element.86, f32[2048]{0:T(1024)S(1)} %get-tuple-element.90, f32[2048]{0:T(1024)S(1)} %get-tuple-element.89, f32[2048]{0:T(1024)S(1)} %rsqrt.34), kind=kLoop, calls=%fused_computation.42 | loop fusion | flops 2621440 | bytes 5267456 | tf_op jit(solution)/shard_map/convert_element_type | solution.py:105
  131.9 1.6 collective-permute-start.8
  133.5 2.3 %collective-permute-start.9 = (bf16[2,64,256]{2,1,0:T(8,128)(2,1)S(1)}, bf16[2,64,256]{2,1,0:T(8,128)(2,1)S(1)}, u32[]{:S(2)}, u32[]{:S(2)}) collective-permute-start(bf16[2,64,256]{2,1,0:T(8,128)(2,1)S(1)} %bitcast.180), channel_id=1, source_target_pairs={{8,0},{16,8},{24,16},{0,24},{9,1},{17,9},{25,17},{1,25},{10,2},{18... | collective-permute-start | bytes 196616 | tf_op jit(solution)/shard_map/ppermute | solution.py:20
  135.8 2.6 %collective-permute-done.8 = bf16[2,64,256]{2,1,0:T(8,128)(2,1)S(1)} collective-permute-done((bf16[2,64,256]{2,1,0:T(8,128)(2,1)S(1)}, bf16[2,64,256]{2,1,0:T(8,128)(2,1)S(1)}, u32[]{:S(2)}, u32[]{:S(2)}) %collective-permute-start.8) | collective-permute-done | bytes 65568 | tf_op jit(solution)/shard_map/ppermute | solution.py:17
  138.6 1.7 collective-permute-start.11
  140.4 1.6 collective-permute-done.10
  142.0 1.1 maximum_select_fusion.2
  143.3 8.8 %fusion.86 = (bf16[32,64,256]{2,1,0:T(8,128)(2,1)S(1)}, f32[32,64,256]{2,1,0:T(8,128)}) fusion(f32[32,64,256]{2,1,0:T(8,128)S(1)} %bitcast.175, bf16[36,68,256]{2,1,0:T(8,128)(2,1)S(1)} %maximum_select_fusion.2, f32[256]{0:T(256)S(1)} %bitcast.197, f32[256]{0:T(256)S(1)} %bitcast.195, f32[256]{0:T(256)S(1)} %bitcast.201, f32[256]{0:T(256)S(1)} %bitcast.203, ...), kind=kLoop, calls=%fused_computation.143 | loop fusion | flops 39845888 | bytes 31482880 | tf_op jit(solution)/shard_map/convert_element_type | solution.py:94
  152.1 6.7 %fusion.21 = (f32[2048]{0:T(1024)S(1)}, f32[2048,256]{1,0:T(8,128)}) fusion(f32[32,64,256]{2,1,0:T(8,128)S(1)} %get-tuple-element.12, f32[256]{0:T(256)} %bitcast.34, bf16[2,256,512]{2,1,0:T(8,128)(2,1)} %param.17, f32[2048,512]{1,0:T(8,128)} %get-tuple-element.82, bf16[2048,256]{1,0:T(8,128)(2,1)S(1)} %bitcast.176, bf16[2,512,256]{2,1,0:T(8,128)(2,1)} %param.18), kind=kOutput, calls=%fused_computation.37 | convolution fusion | flops 1095235584 | bytes 9970688 | tf_op jit(solution)/shard_map/dot_general | solution.py:99
  158.8 2.3 %fusion.20 = bf16[2048,256]{1,0:T(8,128)(2,1)S(1)} fusion(f32[32,64,256]{2,1,0:T(8,128)S(1)} %get-tuple-element.12, f32[2048,256]{1,0:T(8,128)} %get-tuple-element.88, f32[2048]{0:T(1024)S(1)} %broadcast_multiply_fusion, f32[2048]{0:T(1024)S(1)} %multiply_multiply_fusion.2, f32[2048]{0:T(1024)S(1)} %rsqrt.35), kind=kLoop, calls=%fused_computation.36 | loop fusion | flops 2621440 | bytes 5267456 | tf_op jit(solution)/shard_map/convert_element_type | solution.py:105
  161.4 1.1 collective-permute-start.12
  162.5 2.8 %collective-permute-start.13 = (bf16[2,64,256]{2,1,0:T(8,128)(2,1)S(1)}, bf16[2,64,256]{2,1,0:T(8,128)(2,1)S(1)}, u32[]{:S(2)}, u32[]{:S(2)}) collective-permute-start(bf16[2,64,256]{2,1,0:T(8,128)(2,1)S(1)} %bitcast.181), channel_id=1, source_target_pairs={{8,0},{16,8},{24,16},{0,24},{9,1},{17,9},{25,17},{1,25},{10,2},{18... | collective-permute-start | bytes 196616 | tf_op jit(solution)/shard_map/ppermute | solution.py:20
  165.2 2.8 %collective-permute-done.12 = bf16[2,64,256]{2,1,0:T(8,128)(2,1)S(1)} collective-permute-done((bf16[2,64,256]{2,1,0:T(8,128)(2,1)S(1)}, bf16[2,64,256]{2,1,0:T(8,128)(2,1)S(1)}, u32[]{:S(2)}, u32[]{:S(2)}) %collective-permute-start.12) | collective-permute-done | bytes 65568 | tf_op jit(solution)/shard_map/ppermute | solution.py:17
  168.0 0.7 collective-permute-done.13
  168.9 1.6 collective-permute-start.15
  170.5 1.6 collective-permute-done.14
  172.2 1.1 maximum_select_fusion.3
  173.5 9.1 %fusion.16 = f32[1,32,64,256]{3,2,1,0:T(8,128)} fusion(f32[32,64,256]{2,1,0:T(8,128)S(1)} %copy-done.4, bf16[36,68,256]{2,1,0:T(8,128)(2,1)S(1)} %maximum_select_fusion.3, bf16[1,32,64,256]{3,2,1,0:T(8,128)(2,1)S(1)} %copy-done.8, f32[256]{0:T(256)S(1)} %bitcast.237, f32[256]{0:T(256)S(1)} %bitcast.239, f32[256]{0:T(256)S(1)} %bitcast.241, ...), kind=kLoop, calls=%fused_computation.30 | loop fusion | flops 41943040 | bytes 32532480 | tf_op jit(solution)/shard_map/broadcast_in_dim | solution.py:198
  (197 shorter events, 1.6 us)
Async XLA Ops:
  6.5 73.6 %copy-start = (bf16[256,128]{1,0:T(8,128)(2,1)S(1)}, bf16[256,128]{1,0:T(8,128)(2,1)}, u32[]{:S(2)}) copy-start(bf16[256,128]{1,0:T(8,128)(2,1)} %param.19) | copy-start | bytes 196612
  6.5 27.9 %copy-start.2 = (bf16[1,32,64,256]{3,2,1,0:T(8,128)(2,1)S(1)}, bf16[1,32,64,256]{3,2,1,0:T(8,128)(2,1)}, u32[]{:S(2)}) copy-start(bf16[1,32,64,256]{3,2,1,0:T(8,128)(2,1)} %param.12) | copy-start | bytes 3145732
  7.5 22.4 %collective-permute-start = (bf16[2,64,256]{2,1,0:T(8,128)(2,1)S(1)}, bf16[2,64,256]{2,1,0:T(8,128)(2,1)S(1)}, u32[]{:S(2)}, u32[]{:S(2)}) collective-permute-start(bf16[2,64,256]{2,1,0:T(8,128)(2,1)S(1)} %get-tuple-element.27), channel_id=1, source_target_pairs={{0,8},{8,16},{16,24},{24,0},{1,9},{9,17},{17,25},{25,1},{2,10},{10... | collective-permute-start | bytes 196616 | tf_op jit(solution)/shard_map/ppermute | solution.py:17
  10.6 19.4 %collective-permute-start.1 = (bf16[2,64,256]{2,1,0:T(8,128)(2,1)S(1)}, bf16[2,64,256]{2,1,0:T(8,128)(2,1)S(1)}, u32[]{:S(2)}, u32[]{:S(2)}) collective-permute-start(bf16[2,64,256]{2,1,0:T(8,128)(2,1)S(1)} %get-tuple-element.28), channel_id=1, source_target_pairs={{8,0},{16,8},{24,16},{0,24},{9,1},{17,9},{25,17},{1,25},{10,2},{18... | collective-permute-start | bytes 196616 | tf_op jit(solution)/shard_map/ppermute | solution.py:20
  19.5 13.3 %all-to-all-start = ((s32[16,1,64]{2,1,0:T(1,128)}), s32[16,1,64]{2,1,0:T(1,128)S(1)}, u32[]{:S(2)}, u32[]{:S(2)}) async-start(s32[16,1,64]{2,1,0:T(1,128)} %all_to_all.9), calls=%async_computation | async-start | bytes 16384 | tf_op jit(solution)/shard_map/all_to_all | solution.py:157
  23.8 87.5 %all-reduce.2.cloned.1.call-start = ((), (), s32[]{:S(2)}) async-start(), calls=%async_computation.2 | async-start | bytes 1048576 | tf_op jit(solution)/shard_map/psum | solution.py:175
  25.3 18.2 %copy-start.48 = (f32[1,1,256]{2,0,1:T(1,128)}, f32[1,1,256]{2,0,1:T(1,128)S(1)}, u32[]{:S(2)}) copy-start(f32[1,1,256]{2,0,1:T(1,128)S(1)} %get-tuple-element.52) | copy-start | bytes 3076
  25.3 18.2 %copy-start.50 = (f32[1,1,256]{2,0,1:T(1,128)}, f32[1,1,256]{2,0,1:T(1,128)S(1)}, u32[]{:S(2)}) copy-start(f32[1,1,256]{2,0,1:T(1,128)S(1)} %get-tuple-element.53) | copy-start | bytes 3076
  25.3 18.2 %copy-start.52 = (f32[1,1,256]{2,0,1:T(1,128)}, f32[1,1,256]{2,0,1:T(1,128)S(1)}, u32[]{:S(2)}) copy-start(f32[1,1,256]{2,0,1:T(1,128)S(1)} %get-tuple-element.54) | copy-start | bytes 3076
  25.3 18.2 %copy-start.54 = (f32[1,1,256]{2,0,1:T(1,128)}, f32[1,1,256]{2,0,1:T(1,128)S(1)}, u32[]{:S(2)}) copy-start(f32[1,1,256]{2,0,1:T(1,128)S(1)} %get-tuple-element.55) | copy-start | bytes 3076
  25.3 18.2 %copy-start.56 = (f32[1,1,256]{2,0,1:T(1,128)}, f32[1,1,256]{2,0,1:T(1,128)S(1)}, u32[]{:S(2)}) copy-start(f32[1,1,256]{2,0,1:T(1,128)S(1)} %get-tuple-element.56) | copy-start | bytes 3076
  25.3 18.2 %copy-start.58 = (f32[1,1,256]{2,0,1:T(1,128)}, f32[1,1,256]{2,0,1:T(1,128)S(1)}, u32[]{:S(2)}) copy-start(f32[1,1,256]{2,0,1:T(1,128)S(1)} %get-tuple-element.57) | copy-start | bytes 3076
  25.3 18.2 %copy-start.60 = (f32[1,1,256]{2,0,1:T(1,128)}, f32[1,1,256]{2,0,1:T(1,128)S(1)}, u32[]{:S(2)}) copy-start(f32[1,1,256]{2,0,1:T(1,128)S(1)} %get-tuple-element.58) | copy-start | bytes 3076
  25.4 18.2 %copy-start.62 = (f32[1,1,256]{2,0,1:T(1,128)}, f32[1,1,256]{2,0,1:T(1,128)S(1)}, u32[]{:S(2)}) copy-start(f32[1,1,256]{2,0,1:T(1,128)S(1)} %get-tuple-element.59) | copy-start | bytes 3076
  25.4 18.2 %copy-start.64 = (f32[1,1,256]{2,0,1:T(1,128)}, f32[1,1,256]{2,0,1:T(1,128)S(1)}, u32[]{:S(2)}) copy-start(f32[1,1,256]{2,0,1:T(1,128)S(1)} %get-tuple-element.60) | copy-start | bytes 3076
  25.4 18.2 %copy-start.66 = (f32[1,1,256]{2,0,1:T(1,128)}, f32[1,1,256]{2,0,1:T(1,128)S(1)}, u32[]{:S(2)}) copy-start(f32[1,1,256]{2,0,1:T(1,128)S(1)} %get-tuple-element.61) | copy-start | bytes 3076
  25.4 18.2 %copy-start.68 = (f32[1,1,256]{2,0,1:T(1,128)}, f32[1,1,256]{2,0,1:T(1,128)S(1)}, u32[]{:S(2)}) copy-start(f32[1,1,256]{2,0,1:T(1,128)S(1)} %get-tuple-element.62) | copy-start | bytes 3076
  25.4 18.2 %copy-start.70 = (f32[1,1,256]{2,0,1:T(1,128)}, f32[1,1,256]{2,0,1:T(1,128)S(1)}, u32[]{:S(2)}) copy-start(f32[1,1,256]{2,0,1:T(1,128)S(1)} %get-tuple-element.63) | copy-start | bytes 3076
  25.4 18.2 %copy-start.72 = (f32[1,1,256]{2,0,1:T(1,128)}, f32[1,1,256]{2,0,1:T(1,128)S(1)}, u32[]{:S(2)}) copy-start(f32[1,1,256]{2,0,1:T(1,128)S(1)} %get-tuple-element.64) | copy-start | bytes 3076
  25.4 18.2 %copy-start.74 = (f32[1,1,256]{2,0,1:T(1,128)}, f32[1,1,256]{2,0,1:T(1,128)S(1)}, u32[]{:S(2)}) copy-start(f32[1,1,256]{2,0,1:T(1,128)S(1)} %get-tuple-element.65) | copy-start | bytes 3076
  25.4 36.8 %copy-start.9 = (f32[1,1,256]{2,0,1:T(1,128)}, f32[1,1,256]{2,0,1:T(1,128)S(1)}, u32[]{:S(2)}) copy-start(f32[1,1,256]{2,0,1:T(1,128)S(1)} %get-tuple-element.48) | copy-start | bytes 3076
  25.4 36.8 %copy-start.11 = (f32[1,1,256]{2,0,1:T(1,128)}, f32[1,1,256]{2,0,1:T(1,128)S(1)}, u32[]{:S(2)}) copy-start(f32[1,1,256]{2,0,1:T(1,128)S(1)} %get-tuple-element.49) | copy-start | bytes 3076
  25.4 36.8 %copy-start.13 = (f32[1,1,256]{2,0,1:T(1,128)}, f32[1,1,256]{2,0,1:T(1,128)S(1)}, u32[]{:S(2)}) copy-start(f32[1,1,256]{2,0,1:T(1,128)S(1)} %get-tuple-element.50) | copy-start | bytes 3076
  25.5 36.8 %copy-start.15 = (f32[1,1,256]{2,0,1:T(1,128)}, f32[1,1,256]{2,0,1:T(1,128)S(1)}, u32[]{:S(2)}) copy-start(f32[1,1,256]{2,0,1:T(1,128)S(1)} %get-tuple-element.51) | copy-start | bytes 3076
  26.9 35.4 %copy-start.17 = (f32[1,1,256]{2,0,1:T(1,128)}, f32[1,1,256]{2,0,1:T(1,128)S(1)}, u32[]{:S(2)}) copy-start(f32[1,1,256]{2,0,1:T(1,128)S(1)} %get-tuple-element.67) | copy-start | bytes 3076
  26.9 35.4 %copy-start.19 = (f32[1,1,256]{2,0,1:T(1,128)}, f32[1,1,256]{2,0,1:T(1,128)S(1)}, u32[]{:S(2)}) copy-start(f32[1,1,256]{2,0,1:T(1,128)S(1)} %get-tuple-element.78) | copy-start | bytes 3076
  27.8 34.5 %copy-start.21 = (f32[1,1,256]{2,0,1:T(1,128)}, f32[1,1,256]{2,0,1:T(1,128)S(1)}, u32[]{:S(2)}) copy-start(f32[1,1,256]{2,0,1:T(1,128)S(1)} %get-tuple-element.29) | copy-start | bytes 3076
  27.8 34.5 %copy-start.23 = (f32[1,1,256]{2,0,1:T(1,128)}, f32[1,1,256]{2,0,1:T(1,128)S(1)}, u32[]{:S(2)}) copy-start(f32[1,1,256]{2,0,1:T(1,128)S(1)} %get-tuple-element.30) | copy-start | bytes 3076
  27.9 34.5 %copy-start.25 = (f32[1,1,256]{2,0,1:T(1,128)}, f32[1,1,256]{2,0,1:T(1,128)S(1)}, u32[]{:S(2)}) copy-start(f32[1,1,256]{2,0,1:T(1,128)S(1)} %get-tuple-element.31) | copy-start | bytes 3076
  27.9 34.5 %copy-start.27 = (f32[1,1,256]{2,0,1:T(1,128)}, f32[1,1,256]{2,0,1:T(1,128)S(1)}, u32[]{:S(2)}) copy-start(f32[1,1,256]{2,0,1:T(1,128)S(1)} %get-tuple-element.32) | copy-start | bytes 3076
  27.9 34.5 %copy-start.29 = (f32[1,1,256]{2,0,1:T(1,128)}, f32[1,1,256]{2,0,1:T(1,128)S(1)}, u32[]{:S(2)}) copy-start(f32[1,1,256]{2,0,1:T(1,128)S(1)} %get-tuple-element.33) | copy-start | bytes 3076
  27.9 34.5 %copy-start.31 = (f32[1,1,256]{2,0,1:T(1,128)}, f32[1,1,256]{2,0,1:T(1,128)S(1)}, u32[]{:S(2)}) copy-start(f32[1,1,256]{2,0,1:T(1,128)S(1)} %get-tuple-element.34) | copy-start | bytes 3076
  27.9 34.5 %copy-start.33 = (f32[1,1,256]{2,0,1:T(1,128)}, f32[1,1,256]{2,0,1:T(1,128)S(1)}, u32[]{:S(2)}) copy-start(f32[1,1,256]{2,0,1:T(1,128)S(1)} %get-tuple-element.35) | copy-start | bytes 3076
  27.9 34.5 %copy-start.35 = (f32[1,1,256]{2,0,1:T(1,128)}, f32[1,1,256]{2,0,1:T(1,128)S(1)}, u32[]{:S(2)}) copy-start(f32[1,1,256]{2,0,1:T(1,128)S(1)} %get-tuple-element.36) | copy-start | bytes 3076
  27.9 34.5 %copy-start.37 = (f32[1,1,256]{2,0,1:T(1,128)}, f32[1,1,256]{2,0,1:T(1,128)S(1)}, u32[]{:S(2)}) copy-start(f32[1,1,256]{2,0,1:T(1,128)S(1)} %get-tuple-element.37) | copy-start | bytes 3076
  27.9 34.5 %copy-start.38 = (f32[1,1,256]{2,0,1:T(1,128)}, f32[1,1,256]{2,0,1:T(1,128)S(1)}, u32[]{:S(2)}) copy-start(f32[1,1,256]{2,0,1:T(1,128)S(1)} %get-tuple-element.38) | copy-start | bytes 3076
  27.9 34.5 %copy-start.39 = (f32[1,1,256]{2,0,1:T(1,128)}, f32[1,1,256]{2,0,1:T(1,128)S(1)}, u32[]{:S(2)}) copy-start(f32[1,1,256]{2,0,1:T(1,128)S(1)} %get-tuple-element.39) | copy-start | bytes 3076
  27.9 34.5 %copy-start.40 = (f32[1,1,256]{2,0,1:T(1,128)}, f32[1,1,256]{2,0,1:T(1,128)S(1)}, u32[]{:S(2)}) copy-start(f32[1,1,256]{2,0,1:T(1,128)S(1)} %get-tuple-element.40) | copy-start | bytes 3076
  28.0 34.5 %copy-start.41 = (f32[1,1,256]{2,0,1:T(1,128)}, f32[1,1,256]{2,0,1:T(1,128)S(1)}, u32[]{:S(2)}) copy-start(f32[1,1,256]{2,0,1:T(1,128)S(1)} %get-tuple-element.41) | copy-start | bytes 3076
  28.0 34.5 %copy-start.42 = (f32[1,1,256]{2,0,1:T(1,128)}, f32[1,1,256]{2,0,1:T(1,128)S(1)}, u32[]{:S(2)}) copy-start(f32[1,1,256]{2,0,1:T(1,128)S(1)} %get-tuple-element.42) | copy-start | bytes 3076
  28.0 34.5 %copy-start.43 = (f32[1,1,256]{2,0,1:T(1,128)}, f32[1,1,256]{2,0,1:T(1,128)S(1)}, u32[]{:S(2)}) copy-start(f32[1,1,256]{2,0,1:T(1,128)S(1)} %get-tuple-element.43) | copy-start | bytes 3076
  28.0 34.5 %copy-start.44 = (f32[1,1,256]{2,0,1:T(1,128)}, f32[1,1,256]{2,0,1:T(1,128)S(1)}, u32[]{:S(2)}) copy-start(f32[1,1,256]{2,0,1:T(1,128)S(1)} %get-tuple-element.44) | copy-start | bytes 3076
  28.0 34.5 %copy-start.45 = (f32[1,1,256]{2,0,1:T(1,128)}, f32[1,1,256]{2,0,1:T(1,128)S(1)}, u32[]{:S(2)}) copy-start(f32[1,1,256]{2,0,1:T(1,128)S(1)} %get-tuple-element.45) | copy-start | bytes 3076
  28.0 34.5 %copy-start.46 = (f32[1,1,256]{2,0,1:T(1,128)}, f32[1,1,256]{2,0,1:T(1,128)S(1)}, u32[]{:S(2)}) copy-start(f32[1,1,256]{2,0,1:T(1,128)S(1)} %get-tuple-element.46) | copy-start | bytes 3076
  28.0 34.5 %copy-start.47 = (f32[1,1,256]{2,0,1:T(1,128)}, f32[1,1,256]{2,0,1:T(1,128)S(1)}, u32[]{:S(2)}) copy-start(f32[1,1,256]{2,0,1:T(1,128)S(1)} %get-tuple-element.47) | copy-start | bytes 3076
  31.0 3.4 %collective-permute-start.2 = (bf16[36,2,256]{2,1,0:T(2,128)(2,1)S(1)}, bf16[36,2,256]{2,1,0:T(2,128)(2,1)S(1)}, u32[]{:S(2)}, u32[]{:S(2)}) collective-permute-start(bf16[36,2,256]{2,1,0:T(2,128)(2,1)S(1)} %get-tuple-element.19), channel_id=1, source_target_pairs={{0,2},{2,4},{4,6},{6,0},{1,3},{3,5},{5,7},{7,1},{8,10},{10,12},{12... | collective-permute-start | bytes 110600 | tf_op jit(solution)/shard_map/ppermute | solution.py:17
  31.5 3.0 %collective-permute-start.3 = (bf16[36,2,256]{2,1,0:T(2,128)(2,1)S(1)}, bf16[36,2,256]{2,1,0:T(2,128)(2,1)S(1)}, u32[]{:S(2)}, u32[]{:S(2)}) collective-permute-start(bf16[36,2,256]{2,1,0:T(2,128)(2,1)S(1)} %get-tuple-element.20), channel_id=1, source_target_pairs={{2,0},{4,2},{6,4},{0,6},{3,1},{5,3},{7,5},{1,7},{10,8},{12,10},{14... | collective-permute-start | bytes 110600 | tf_op jit(solution)/shard_map/ppermute | solution.py:20
  48.8 6.2 %collective-permute-start.4 = (bf16[2,64,256]{2,1,0:T(8,128)(2,1)S(1)}, bf16[2,64,256]{2,1,0:T(8,128)(2,1)S(1)}, u32[]{:S(2)}, u32[]{:S(2)}) collective-permute-start(bf16[2,64,256]{2,1,0:T(8,128)(2,1)S(1)} %get-tuple-element.25), channel_id=1, source_target_pairs={{0,8},{8,16},{16,24},{24,0},{1,9},{9,17},{17,25},{25,1},{2,10},{10... | collective-permute-start | bytes 196616 | tf_op jit(solution)/shard_map/ppermute | solution.py:17
  50.8 6.2 %collective-permute-start.5 = (bf16[2,64,256]{2,1,0:T(8,128)(2,1)S(1)}, bf16[2,64,256]{2,1,0:T(8,128)(2,1)S(1)}, u32[]{:S(2)}, u32[]{:S(2)}) collective-permute-start(bf16[2,64,256]{2,1,0:T(8,128)(2,1)S(1)} %get-tuple-element.26), channel_id=1, source_target_pairs={{8,0},{16,8},{24,16},{0,24},{9,1},{17,9},{25,17},{1,25},{10,2},{18... | collective-permute-start | bytes 196616 | tf_op jit(solution)/shard_map/ppermute | solution.py:20
  57.1 3.4 %collective-permute-start.6 = (bf16[36,2,256]{2,1,0:T(2,128)(2,1)S(1)}, bf16[36,2,256]{2,1,0:T(2,128)(2,1)S(1)}, u32[]{:S(2)}, u32[]{:S(2)}) collective-permute-start(bf16[36,2,256]{2,1,0:T(2,128)(2,1)S(1)} %get-tuple-element.17), channel_id=1, source_target_pairs={{0,2},{2,4},{4,6},{6,0},{1,3},{3,5},{5,7},{7,1},{8,10},{10,12},{12... | collective-permute-start | bytes 110600 | tf_op jit(solution)/shard_map/ppermute | solution.py:17
  57.3 3.3 %collective-permute-start.7 = (bf16[36,2,256]{2,1,0:T(2,128)(2,1)S(1)}, bf16[36,2,256]{2,1,0:T(2,128)(2,1)S(1)}, u32[]{:S(2)}, u32[]{:S(2)}) collective-permute-start(bf16[36,2,256]{2,1,0:T(2,128)(2,1)S(1)} %get-tuple-element.18), channel_id=1, source_target_pairs={{2,0},{4,2},{6,4},{0,6},{3,1},{5,3},{7,5},{1,7},{10,8},{12,10},{14... | collective-permute-start | bytes 110600 | tf_op jit(solution)/shard_map/ppermute | solution.py:20
  80.1 31.2 %copy-start.77 = (f32[128]{0:T(128)S(1)}, f32[128]{0:T(128)}, u32[]{:S(2)}) copy-start(f32[128]{0:T(128)} %param.20) | copy-start | bytes 1540
  85.2 14.8 %all-to-all-start.1 = ((bf16[16,64,128]{2,1,0:T(8,128)(2,1)}), bf16[16,64,128]{2,1,0:T(8,128)(2,1)S(1)}, u32[]{:S(2)}, u32[]{:S(2)}) async-start(bf16[16,64,128]{2,1,0:T(8,128)(2,1)} %bitcast.72), calls=%async_computation.1 | async-start | bytes 524288 | tf_op jit(solution)/shard_map/all_to_all | solution.py:150
  131.9 6.6 %collective-permute-start.8 = (bf16[2,64,256]{2,1,0:T(8,128)(2,1)S(1)}, bf16[2,64,256]{2,1,0:T(8,128)(2,1)S(1)}, u32[]{:S(2)}, u32[]{:S(2)}) collective-permute-start(bf16[2,64,256]{2,1,0:T(8,128)(2,1)S(1)} %bitcast.182), channel_id=1, source_target_pairs={{0,8},{8,16},{16,24},{24,0},{1,9},{9,17},{17,25},{25,1},{2,10},{10... | collective-permute-start | bytes 196616 | tf_op jit(solution)/shard_map/ppermute | solution.py:17
  133.5 5.0 %collective-permute-start.9 = (bf16[2,64,256]{2,1,0:T(8,128)(2,1)S(1)}, bf16[2,64,256]{2,1,0:T(8,128)(2,1)S(1)}, u32[]{:S(2)}, u32[]{:S(2)}) collective-permute-start(bf16[2,64,256]{2,1,0:T(8,128)(2,1)S(1)} %bitcast.180), channel_id=1, source_target_pairs={{8,0},{16,8},{24,16},{0,24},{9,1},{17,9},{25,17},{1,25},{10,2},{18... | collective-permute-start | bytes 196616 | tf_op jit(solution)/shard_map/ppermute | solution.py:20
  138.6 3.4 %collective-permute-start.10 = (bf16[36,2,256]{2,1,0:T(2,128)(2,1)S(1)}, bf16[36,2,256]{2,1,0:T(2,128)(2,1)S(1)}, u32[]{:S(2)}, u32[]{:S(2)}) collective-permute-start(bf16[36,2,256]{2,1,0:T(2,128)(2,1)S(1)} %get-tuple-element.15), channel_id=1, source_target_pairs={{0,2},{2,4},{4,6},{6,0},{1,3},{3,5},{5,7},{7,1},{8,10},{10,12},{12... | collective-permute-start | bytes 110600 | tf_op jit(solution)/shard_map/ppermute | solution.py:17
  138.6 3.4 %collective-permute-start.11 = (bf16[36,2,256]{2,1,0:T(2,128)(2,1)S(1)}, bf16[36,2,256]{2,1,0:T(2,128)(2,1)S(1)}, u32[]{:S(2)}, u32[]{:S(2)}) collective-permute-start(bf16[36,2,256]{2,1,0:T(2,128)(2,1)S(1)} %get-tuple-element.16), channel_id=1, source_target_pairs={{2,0},{4,2},{6,4},{0,6},{3,1},{5,3},{7,5},{1,7},{10,8},{12,10},{14... | collective-permute-start | bytes 110600 | tf_op jit(solution)/shard_map/ppermute | solution.py:20
  158.8 14.5 %copy-start.8 = (bf16[1,32,64,256]{3,2,1,0:T(8,128)(2,1)S(1)}, bf16[1,32,64,256]{3,2,1,0:T(8,128)(2,1)}, u32[]{:S(2)}) copy-start(bf16[1,32,64,256]{3,2,1,0:T(8,128)(2,1)} %param.13) | copy-start | bytes 3145732
  161.2 12.2 %copy-start.3 = (bf16[1,32,64,256]{3,2,1,0:T(8,128)(2,1)S(1)}, bf16[1,32,64,256]{3,2,1,0:T(8,128)(2,1)}, u32[]{:S(2)}) copy-start(bf16[1,32,64,256]{3,2,1,0:T(8,128)(2,1)} %param.12) | copy-start | bytes 3145732
  161.2 12.2 %copy-start.4 = (f32[32,64,256]{2,1,0:T(8,128)S(1)}, f32[32,64,256]{2,1,0:T(8,128)}, u32[]{:S(2)}) copy-start(f32[32,64,256]{2,1,0:T(8,128)} %get-tuple-element.8) | copy-start | bytes 6291460
  161.4 6.7 %collective-permute-start.12 = (bf16[2,64,256]{2,1,0:T(8,128)(2,1)S(1)}, bf16[2,64,256]{2,1,0:T(8,128)(2,1)S(1)}, u32[]{:S(2)}, u32[]{:S(2)}) collective-permute-start(bf16[2,64,256]{2,1,0:T(8,128)(2,1)S(1)} %bitcast.183), channel_id=1, source_target_pairs={{0,8},{8,16},{16,24},{24,0},{1,9},{9,17},{17,25},{25,1},{2,10},{10... | collective-permute-start | bytes 196616 | tf_op jit(solution)/shard_map/ppermute | solution.py:17
  162.5 6.2 %collective-permute-start.13 = (bf16[2,64,256]{2,1,0:T(8,128)(2,1)S(1)}, bf16[2,64,256]{2,1,0:T(8,128)(2,1)S(1)}, u32[]{:S(2)}, u32[]{:S(2)}) collective-permute-start(bf16[2,64,256]{2,1,0:T(8,128)(2,1)S(1)} %bitcast.181), channel_id=1, source_target_pairs={{8,0},{16,8},{24,16},{0,24},{9,1},{17,9},{25,17},{1,25},{10,2},{18... | collective-permute-start | bytes 196616 | tf_op jit(solution)/shard_map/ppermute | solution.py:20
  168.7 3.4 %collective-permute-start.14 = (bf16[36,2,256]{2,1,0:T(2,128)(2,1)S(1)}, bf16[36,2,256]{2,1,0:T(2,128)(2,1)S(1)}, u32[]{:S(2)}, u32[]{:S(2)}) collective-permute-start(bf16[36,2,256]{2,1,0:T(2,128)(2,1)S(1)} %get-tuple-element.13), channel_id=1, source_target_pairs={{0,2},{2,4},{4,6},{6,0},{1,3},{3,5},{5,7},{7,1},{8,10},{10,12},{12... | collective-permute-start | bytes 110600 | tf_op jit(solution)/shard_map/ppermute | solution.py:17
  168.9 3.3 %collective-permute-start.15 = (bf16[36,2,256]{2,1,0:T(2,128)(2,1)S(1)}, bf16[36,2,256]{2,1,0:T(2,128)(2,1)S(1)}, u32[]{:S(2)}, u32[]{:S(2)}) collective-permute-start(bf16[36,2,256]{2,1,0:T(2,128)(2,1)S(1)} %get-tuple-element.14), channel_id=1, source_target_pairs={{2,0},{4,2},{6,4},{0,6},{3,1},{5,3},{7,5},{1,7},{10,8},{12,10},{14... | collective-permute-start | bytes 110600 | tf_op jit(solution)/shard_map/ppermute | solution.py:20
  (37 other events, 375.0 us)
Sparse Core Ops, SparseCore 0:
  82.5 28.7 all-reduce.1
where the time goes:
time: 191 us; the launch traced here: 189 us
  other arithmetic  57.8 us (30%)
  waiting for transfers between devices  37.9 us (20%)
  starting transfers between devices  33.1 us (17%)
  matrix products  26.7 us (14%)
  local copies, waits for them, and re-layouts  19.2 us (10%)
  between operations  14.8 us (8%)
    ppermute x8, starting transfers between devices, extended(): lax.ppermute(lax.slice_in_dim(block, 0, width, axis=dim), axis, backward)  15.4 us
    reduce_sum x2, other arithmetic, layer_front(): jnp.mean(flat_conv * flat_conv, axis=1, keepdims=True) + EPSILON  14.9 us
    dot_general x2, matrix products, layer_back(): jnp.dot(hidden_grad, layer_in.T, preferred_element_type=jnp.float32)  14.9 us
    ppermute x8, waiting for transfers between devices, extended(): lax.ppermute(lax.slice_in_dim(block, block.shape[dim] - width, None, axis...  13.9 us
    psum x1, waiting for transfers between devices, per_device(): ensemble_sum = lax.psum(predicted, 'ens')  11.3 us
    all_to_all x1, waiting for transfers between devices, per_device(): lax.all_to_all(send_values.reshape(grid_count, capacity, obs_channels), (...  9.98 us
    broadcast_in_dim x1, other arithmetic, per_device(): return (prior + upstream)[None]  9.12 us
    convert_element_type x1, other arithmetic, layer_back(): upstream.reshape(-1, channels).astype(jnp.bfloat16)  8.79 us
  transfers between devices with their start and end apart: 19, of which 11 were waited for; matrix products, arithmetic and copies ran while one was open for 9% of the time, Pallas kernels for 0%

commit v1 on v0

v1 whole, which is shorter than its diff:
```python
import functools

import jax
import jax.numpy as jnp
from jax import lax
from jax.experimental import pallas as pl
from jax.experimental.pallas import tpu as pltpu
from jax.sharding import PartitionSpec as P

SQRT_TWO_OVER_PI = 0.7978845608
CUBIC = 0.044715
EPSILON = 1e-06
LANES = 128
ROWS = 8
VMEM_BYTES = 56 * 1024 * 1024


def dot(a, b):
    return jnp.dot(a, b, preferred_element_type=jnp.float32)


def dot_t(a, b):
    return lax.dot_general(a, b, (((1,), (1,)), ((), ())), preferred_element_type=jnp.float32)


def shifted_copies(x, up, down, left, right, xp, xs):
    height, width, _ = x.shape
    xp[0:2, 8 : 8 + width] = up[...].astype(jnp.float32)
    xp[height + 2 : height + 4, 8 : 8 + width] = down[...].astype(jnp.float32)
    xp[:, 6:8] = left[...].astype(jnp.float32)
    xp[:, 8 + width : 10 + width] = right[...].astype(jnp.float32)

    def fill(step, carry):
        r = step * 4
        xp[pl.ds(r + 2, 4), 8 : 8 + width] = x[pl.ds(r, 4)].astype(jnp.float32)
        return carry

    lax.fori_loop(0, height // 4, fill, 0)

    def shift(step, carry):
        r = step * 4
        for j in range(5):
            xs[j, pl.ds(r, 4)] = xp[pl.ds(r, 4), 6 + j : 6 + j + width]
        return carry

    lax.fori_loop(0, (height + 4) // 4, shift, 0)


def conv_rows(xs, taps, out, r0):
    width, channels = xs.shape[2], xs.shape[3]

    def column(step, carry):
        c0 = pl.multiple_of(step * 8, 8)
        for part in range(channels // LANES):
            lanes = slice(part * LANES, (part + 1) * LANES)
            acc = None
            for j in range(5):
                xj = xs[j, pl.ds(r0, ROWS + 4), pl.ds(c0, 8), lanes]
                for i in range(5):
                    tap = taps[5 * i + j : 5 * i + j + 1, lanes][None]
                    term = tap * xj[i : i + ROWS]
                    acc = term if acc is None else acc + term
            out[:, pl.ds(c0, 8), lanes] = acc
        return carry

    lax.fori_loop(0, width // 8, column, 0)


def forward_block(h, x, gain, w_in, w_out):
    s = lax.rsqrt(jnp.mean(h * h, axis=1, keepdims=True) + EPSILON)
    n = (h * s * gain).astype(jnp.bfloat16)
    z = dot(n, w_in)
    zz = z * z
    inner = jnp.tanh(z * (SQRT_TWO_OVER_PI + (SQRT_TWO_OVER_PI * CUBIC) * zz))
    half = 0.5 + 0.5 * inner
    t = (z * half).astype(jnp.bfloat16)
    slope = half + (z * (0.5 - 0.5 * inner * inner)) * (
        SQRT_TWO_OVER_PI + (SQRT_TWO_OVER_PI * 3.0 * CUBIC) * zz
    )
    mixed = dot(t, w_out)
    return s, n, slope.astype(jnp.bfloat16), (x.astype(jnp.float32) + mixed).astype(jnp.bfloat16)


def backward_block(g, n, s, slope, gain, w_in, w_out):
    u = dot_t(g.astype(jnp.bfloat16), w_out)
    dz = (u * slope.astype(jnp.float32)).astype(jnp.bfloat16)
    dn = dot_t(dz, w_in)
    nf = n.astype(jnp.float32)
    m = jnp.mean(dn * nf, axis=1, keepdims=True)
    return (s * (gain * dn - (nf * (1.0 / gain)) * m)).astype(jnp.bfloat16)


def forward_layer(x, up, down, left, right, taps, gain, w_in, w_out, nxt, n_out, s_out, slope_out, xp, xs, hb):
    height, width, channels = x.shape
    shifted_copies(x, up, down, left, right, xp, xs)

    def block(step, carry):
        r0 = step * ROWS
        conv_rows(xs, taps, hb, r0)
        cells = ROWS * width
        flat = pl.ds(pl.multiple_of(step * cells, cells), cells)
        s, n, slope, new = forward_block(
            hb[...].reshape(cells, channels),
            x[pl.ds(r0, ROWS)].reshape(cells, channels),
            gain[...],
            w_in[...],
            w_out[...],
        )
        nxt[pl.ds(r0, ROWS)] = new.reshape(ROWS, width, channels)
        n_out[flat] = n
        s_out[flat] = jnp.broadcast_to(s, (cells, LANES))
        slope_out[flat] = slope
        return carry

    lax.fori_loop(0, height // ROWS, block, 0)


def first_kernel(*refs):
    forward_layer(*refs)


def second_kernel(x, up, down, left, right, taps, gain, w_in, w_out, cells_col, op, n_out, s_out, slope_out, pred, xp, xs, hb, last):
    forward_layer(x, up, down, left, right, taps, gain, w_in, w_out, last, n_out, s_out, slope_out, xp, xs, hb)
    height, width, channels = x.shape
    cells = height * width
    chunk = 256
    state = last[...].reshape(cells, channels)

    def gather(step, carry):
        at = pl.ds(pl.multiple_of(step * chunk, chunk), chunk)
        where = lax.broadcasted_iota(jnp.int32, (chunk, cells), 1)
        hot = (where == cells_col[at]).astype(jnp.float32).astype(jnp.bfloat16)
        rows = dot(hot, state).astype(jnp.bfloat16)
        pred[at] = dot(rows, op[...])
        return carry

    lax.fori_loop(0, cells_col.shape[0] // chunk, gather, 0)


def adjoint_kernel(members, mine, other, values, cells_row, op, precision, n_in, s_in, slope_in, gain, w_in, w_out, g_out, dh_out):
    width = dh_out.shape[1]
    slots = mine.shape[0]
    mean_pred = (mine[...] + other[...]) * (1.0 / members)
    adj = (precision[...] * (mean_pred - values[...].astype(jnp.float32)) * (1.0 / members)).astype(jnp.bfloat16)
    cells = ROWS * width

    def block(step, carry):
        flat = pl.ds(pl.multiple_of(step * cells, cells), cells)
        where = lax.broadcasted_iota(jnp.int32, (cells, slots), 0) + step * cells
        hot = (where == cells_row[...]).astype(jnp.float32).astype(jnp.bfloat16)
        total = dot(hot, adj)
        high = total.astype(jnp.bfloat16)
        low = (total - high.astype(jnp.float32)).astype(jnp.bfloat16)
        g = dot_t(high, op[...]) + dot_t(low, op[...])
        g_out[flat] = g
        dh = backward_block(
            g, n_in[flat], s_in[flat][:, 0:1], slope_in[flat], gain[...], w_in[...], w_out[...]
        )
        dh_out[pl.ds(step * ROWS, ROWS)] = dh.reshape(ROWS, width, dh.shape[1])
        return carry

    lax.fori_loop(0, dh_out.shape[0] // ROWS, block, 0)


def middle_kernel(dh, up, down, left, right, taps, g_in, n_in, s_in, slope_in, gain, w_in, w_out, g_out, dh_out, xp, xs, hb):
    height, width, channels = dh.shape
    shifted_copies(dh, up, down, left, right, xp, xs)
    cells = ROWS * width

    def block(step, carry):
        r0 = step * ROWS
        conv_rows(xs, taps, hb, r0)
        flat = pl.ds(pl.multiple_of(step * cells, cells), cells)
        g = g_in[flat] + hb[...].reshape(cells, channels)
        g_out[flat] = g
        new = backward_block(
            g, n_in[flat], s_in[flat][:, 0:1], slope_in[flat], gain[...], w_in[...], w_out[...]
        )
        dh_out[pl.ds(r0, ROWS)] = new.reshape(ROWS, width, channels)
        return carry

    lax.fori_loop(0, height // ROWS, block, 0)


def last_kernel(dh, up, down, left, right, taps, g_in, x, background, precision, out, xp, xs, hb):
    height, width, channels = dh.shape
    shifted_copies(dh, up, down, left, right, xp, xs)
    cells = ROWS * width

    def block(step, carry):
        r0 = step * ROWS
        conv_rows(xs, taps, hb, r0)
        flat = pl.ds(pl.multiple_of(step * cells, cells), cells)
        rows = pl.ds(r0, ROWS)
        diff = x[rows].astype(jnp.float32) - background[rows].astype(jnp.float32)
        prior = precision[...] * diff.reshape(cells, channels)
        out[rows] = (prior + (g_in[flat] + hb[...].reshape(cells, channels))).reshape(ROWS, width, channels)
        return carry

    lax.fori_loop(0, height // ROWS, block, 0)


def call(kernel, outs, args, scratch=(), flops=0):
    whole = pl.BlockSpec(memory_space=pltpu.VMEM)
    moved = sum(a.size * a.dtype.itemsize for a in args) + sum(o.size * o.dtype.itemsize for o in outs)
    return pl.pallas_call(
        kernel,
        out_shape=list(outs),
        in_specs=[whole] * len(args),
        out_specs=[whole] * len(outs),
        scratch_shapes=list(scratch),
        compiler_params=pltpu.CompilerParams(vmem_limit_bytes=VMEM_BYTES),
        cost_estimate=pl.CostEstimate(flops=flops, bytes_accessed=moved, transcendentals=0),
    )(*args)


def halos(field):
    height, width, _ = field.shape
    lat = lax.axis_size("lat")
    lon = lax.axis_size("lon")
    up_perm = [(i, i + 1) for i in range(lat - 1)]
    down_perm = [(i + 1, i) for i in range(lat - 1)]
    up = lax.ppermute(field[height - 2 :], "lat", up_perm)
    down = lax.ppermute(field[:2], "lat", down_perm)
    right_edge = jnp.concatenate([up[:, width - 2 :], field[:, width - 2 :], down[:, width - 2 :]], axis=0)
    left_edge = jnp.concatenate([up[:, :2], field[:, :2], down[:, :2]], axis=0)
    left = lax.ppermute(right_edge, "lon", [(i, (i + 1) % lon) for i in range(lon)])
    right = lax.ppermute(left_edge, "lon", [((i + 1) % lon, i) for i in range(lon)])
    return up, down, left, right


def route(obs_values, obs_owner, obs_cell, grid_count, capacity):
    count, channels = obs_values.shape
    bf16 = jnp.bfloat16
    owner = obs_owner[:, 0]
    hits = owner[:, None] == jnp.arange(grid_count, dtype=jnp.int32)[None, :]
    order = jnp.arange(count, dtype=jnp.int32)
    earlier = dot((order[None, :] < order[:, None]).astype(bf16), hits.astype(bf16))
    rank = jnp.sum(jnp.where(hits, earlier, 0.0), axis=1).astype(jnp.int32)
    slot = owner * capacity + rank
    slots = grid_count * capacity
    hot = (jnp.arange(slots, dtype=jnp.int32)[:, None] == slot[None, :]).astype(bf16)
    send_values = dot(hot, obs_values).astype(bf16)
    cell_parts = jnp.stack([obs_cell // 64, obs_cell % 64, jnp.ones_like(obs_cell)], axis=1).astype(bf16)
    parts = dot(hot, cell_parts).astype(jnp.int32)
    send_cells = parts[:, 0] * 64 + parts[:, 1] + parts[:, 2] - 1
    axes = ("lat", "lon")
    values = lax.all_to_all(
        send_values.reshape(grid_count, capacity, channels), axes, split_axis=0, concat_axis=0, tiled=True
    )
    cells = lax.all_to_all(
        send_cells.reshape(grid_count, capacity), axes, split_axis=0, concat_axis=0, tiled=True
    )
    return values.reshape(slots, channels), cells.reshape(slots)


def per_device(
    initial_state,
    background,
    background_precision,
    kernel_taps,
    norm_gains,
    weight_in,
    weight_out,
    obs_operator,
    obs_precision,
    obs_values,
    obs_owner,
    obs_cell,
):
    f32, bf16 = jnp.float32, jnp.bfloat16
    shape = jax.ShapeDtypeStruct
    start = initial_state[0]
    height, width, channels = start.shape
    hidden = weight_in.shape[2]
    cells = height * width
    obs_channels = obs_values.shape[1]
    members = lax.axis_size("ens")
    grid_count = lax.axis_size("lat") * lax.axis_size("lon")
    capacity = 2 * obs_values.shape[0] // grid_count
    slots = grid_count * capacity
    values, got_cells = route(obs_values, obs_owner, obs_cell, grid_count, capacity)

    conv_scratch = [
        pltpu.VMEM((height + 4, width + 16, channels), f32),
        pltpu.VMEM((5, height + 4, width, channels), f32),
        pltpu.VMEM((ROWS, width, channels), f32),
    ]
    state_shape = shape((height, width, channels), bf16)
    kept = [shape((cells, channels), bf16), shape((cells, LANES), f32), shape((cells, hidden), bf16)]
    conv_flops = 50 * cells * channels
    mix_flops = 4 * cells * channels * hidden
    gains = norm_gains[:, None, :]
    reverse = kernel_taps[:, ::-1]

    middle, n1, s1, slope1 = call(
        first_kernel,
        [state_shape] + kept,
        [start, *halos(start), kernel_taps[0], gains[0], weight_in[0], weight_out[0]],
        conv_scratch,
        conv_flops + mix_flops,
    )
    n2, s2, slope2, pred = call(
        second_kernel,
        kept + [shape((slots, obs_channels), f32)],
        [middle, *halos(middle), kernel_taps[1], gains[1], weight_in[1], weight_out[1], got_cells[:, None], obs_operator],
        conv_scratch + [pltpu.VMEM((height, width, channels), bf16)],
        conv_flops + mix_flops,
    )
    if members == 2:
        other = lax.ppermute(pred, "ens", [(0, 1), (1, 0)])
    else:
        other = lax.psum(pred, "ens") - pred
    g2, dh2 = call(
        functools.partial(adjoint_kernel, members),
        [shape((cells, channels), f32), state_shape],
        [pred, other, values, got_cells[None, :], obs_operator, obs_precision[None, :], n2, s2, slope2, gains[1], weight_in[1], weight_out[1]],
        (),
        mix_flops,
    )
    g1, dh1 = call(
        middle_kernel,
        [shape((cells, channels), f32), state_shape],
        [dh2, *halos(dh2), reverse[1], g2, n1, s1, slope1, gains[0], weight_in[0], weight_out[0]],
        conv_scratch,
        conv_flops + mix_flops,
    )
    (out,) = call(
        last_kernel,
        [shape((height, width, channels), f32)],
        [dh1, *halos(dh1), reverse[0], g1, start, background[0], background_precision[None, :]],
        conv_scratch,
        conv_flops,
    )
    return out[None]


def solution(mesh):
    in_specs = (
        P("ens", "lat", "lon", None),
        P("ens", "lat", "lon", None),
        P(),
        P(),
        P(),
        P(),
        P(),
        P(),
        P(),
        P(("lat", "lon"), None),
        P(("lat", "lon"), None),
        P(("lat", "lon")),
    )
    out_specs = P("ens", "lat", "lon", None)
    return jax.shard_map(
        per_device, mesh=mesh, in_specs=in_specs, out_specs=out_specs, check_vma=False
    )
```

time: 191 us -> 154 us (0.81)
  Pallas kernels: 0 us -> 58.5 us
  other arithmetic: 57.8 us -> 2.52 us
  matrix products: 26.7 us -> 2.66 us
  between operations: 14.8 us -> 0.41 us
  waiting for transfers between devices: 37.9 us -> 23.6 us
  starting transfers between devices: 33.1 us -> 44.4 us
    pallas_call x0 -> x5, Pallas kernels: none -> 58.5 us  [call(): pl.pallas_call(kernel, out_shape=list(outs), in_specs=[whole] * len(args)...]
    dot_general x8 -> x3, matrix products: 26.7 us -> 2.66 us  [dot(): return jnp.dot(a, b, preferred_element_type=jnp.float32)]
    convert_element_type x6 -> x0, other arithmetic: 15.9 us -> none  [the longest x1 8.79 us: layer_back(): upstream.reshape(-1, channels).astype(jnp.bfloat16)]
    reduce_sum x3 -> x0, other arithmetic: 15.7 us -> none  [the longest x2 14.9 us: layer_front(): jnp.mean(flat_conv * flat_conv, axis=1, keepdims=True) + EPSILON]
    psum x1 -> x0, waiting for transfers between devices: 11.3 us -> none  [per_device(): ensemble_sum = lax.psum(predicted, 'ens')]
    ppermute x16 -> x17, starting transfers between devices: 24 us -> 33.6 us  [the longest x4 19.6 us: halos(): up = lax.ppermute(field[height - 2:], 'lat', up_perm)]
    broadcast_in_dim x1 -> x0, other arithmetic: 9.12 us -> none  [per_device(): return (prior + upstream)[None]]
    scatter-add x1 -> x0, other arithmetic: 8.19 us -> none  [per_device(): upstream = jnp.zeros((height * width, channels), jnp.float32).at[cell_saf...]
  transfers between devices with their start and end apart: 19 -> 19, of which waited for: 11 -> 9; matrix products, arithmetic and copies ran while one was open for 9% -> 12% of each run, Pallas kernels for 0% -> 0%
where the time goes in v1:
time: 154 us; the launch traced here: 153 us
  Pallas kernels  58.5 us (38%)
  starting transfers between devices  44.4 us (29%)
  waiting for transfers between devices  23.6 us (15%)
  local copies, waits for them, and re-layouts  21 us (14%)
  matrix products  2.66 us (2%)
  other arithmetic  2.52 us (2%)
    pallas_call x5, Pallas kernels, call(): pl.pallas_call(kernel, out_shape=list(outs), in_specs=[whole] * len(args)...  58.5 us
    ppermute x4, starting transfers between devices, halos(): up = lax.ppermute(field[height - 2:], 'lat', up_perm)  19.6 us
    all_to_all x1, waiting for transfers between devices, route(): lax.all_to_all(send_values.reshape(grid_count, capacity, channels), axes,...  9.34 us
    all_to_all x1, starting transfers between devices, route(): lax.all_to_all(send_cells.reshape(grid_count, capacity), axes, split_axis...  7.24 us
    ppermute x4, starting transfers between devices, halos(): lax.ppermute(left_edge, 'lon', [((i + 1) % lon, i) for i in range(lon)])  6.22 us
    all_to_all x1, waiting for transfers between devices, route(): lax.all_to_all(send_cells.reshape(grid_count, capacity), axes, split_axis...  5.79 us
    ppermute x4, waiting for transfers between devices, halos(): up = lax.ppermute(field[height - 2:], 'lat', up_perm)  5.55 us
    ppermute x4, starting transfers between devices, halos(): down = lax.ppermute(field[:2], 'lat', down_perm)  5.17 us
  transfers between devices with their start and end apart: 19, of which 9 were waited for; matrix products, arithmetic and copies ran while one was open for 12% of the time, Pallas kernels for 0%

profile of v1, /device:TPU:0, one launch (start us, length us, event | category | flops | bytes accessed | tf_op | source)
XLA Modules:
  0.0 153.1 jit_solution(3234080597780025798)
XLA Ops:
  0.0 0.9 slice_bitcast_fusion.4
  1.0 1.3 collective-permute-start.1
  2.3 5.6 %collective-permute-start = (bf16[2,64,256]{2,1,0:T(8,128)(2,1)S(1)}, bf16[2,64,256]{2,1,0:T(8,128)(2,1)S(1)}, u32[]{:S(2)}, u32[]{:S(2)}) collective-permute-start(bf16[2,64,256]{2,1,0:T(8,128)(2,1)S(1)} %get-tuple-element.44), channel_id=1, source_target_pairs={{0,8},{8,16},{16,24},{1,9},{9,17},{17,25},{2,10},{10,18},{18,26},{... | collective-permute-start | bytes 196616 | tf_op jit(solution)/shard_map/ppermute | solution.py:223
  7.8 1.0 fusion.3
  8.9 0.7 convert_add_fusion
  9.5 0.7 fusion.15
  10.3 0.9 fusion.34
  11.2 1.0 fusion.25
  12.2 1.9 %slice_bitcast_fusion.1 = (bf16[256,512]{1,0:T(8,128)(2,1)}, bf16[256,512]{1,0:T(8,128)(2,1)}) fusion(bf16[2,256,512]{2,1,0:T(8,128)(2,1)} %param.17), kind=kLoop, calls=%fused_computation.11 | loop fusion | bytes 1048576 | tf_op jit(solution)/shard_map/squeeze | solution.py:306
  14.1 0.8 slice_bitcast_fusion
  14.9 0.1 pad.14.clone
  15.0 0.5 fusion.4
  15.7 1.8 %collective-permute-start.3 = (bf16[36,2,256]{2,1,0:T(2,128)(2,1)S(1)}, bf16[36,2,256]{2,1,0:T(2,128)(2,1)S(1)}, u32[]{:S(2)}, u32[]{:S(2)}) collective-permute-start(bf16[36,2,256]{2,1,0:T(2,128)(2,1)S(1)} %pad_maximum_fusion.1), channel_id=1, source_target_pairs={{2,0},{4,2},{6,4},{0,6},{3,1},{5,3},{7,5},{1,7},{10,8},{12,10},{14... | collective-permute-start | bytes 110600 | tf_op jit(solution)/shard_map/ppermute | solution.py:228
  17.5 0.6 fusion.37
  18.1 0.6 copy.28
  18.7 0.3 collective-permute-done.2.refs_3_
  19.0 0.1 collective-permute-done.3.refs_4_
  19.1 0.5 copy-done.21
  19.6 0.1 copy-done.22
  19.7 12.0 %shard_map.118 = (bf16[32,64,256]{2,1,0:T(8,128)(2,1)}, bf16[2048,256]{1,0:T(8,128)(2,1)}, f32[2048,128]{1,0:T(8,128)}, bf16[2048,512]{1,0:T(8,128)(2,1)}) custom-call(bf16[32,64,256]{2,1,0:T(8,128)(2,1)} %bitcast.31, bf16[2,64,256]{2,1,0:T(8,128)(2,1)} %copy-done.16, bf16[2,64,256]{2,1,0:T(8,128)(2,1)} %copy-done.15, bf16[36,2,256]{2,1,0:T(2,128)(2,1)} %copy-done.21, ...), custom_call_target="tpu_custom_call" | custom-call | flops 1099956224 | bytes 7047168 | tf_op jit(solution)/shard_map/pallas_call | solution.py:206
  31.7 0.9 fusion.24
  32.6 1.3 collective-permute-start.5
  33.9 1.0 fusion.23
  34.9 4.6 %collective-permute-start.4 = (bf16[2,64,256]{2,1,0:T(8,128)(2,1)S(1)}, bf16[2,64,256]{2,1,0:T(8,128)(2,1)S(1)}, u32[]{:S(2)}, u32[]{:S(2)}) collective-permute-start(bf16[2,64,256]{2,1,0:T(8,128)(2,1)S(1)} %get-tuple-element.40), channel_id=1, source_target_pairs={{0,8},{8,16},{16,24},{1,9},{9,17},{17,25},{2,10},{10,18},{18,26},{... | collective-permute-start | bytes 196616 | tf_op jit(solution)/shard_map/ppermute | solution.py:223
  39.5 1.8 %collective-permute-done.4.up = bf16[2,64,256]{2,1,0:T(8,128)(2,1)S(1)} collective-permute-done((bf16[2,64,256]{2,1,0:T(8,128)(2,1)S(1)}, bf16[2,64,256]{2,1,0:T(8,128)(2,1)S(1)}, u32[]{:S(2)}, u32[]{:S(2)}) %collective-permute-start.4) | collective-permute-done | bytes 65568 | tf_op jit(solution)/shard_map/ppermute | solution.py:223
  41.4 1.0 collective-permute-start.6
  42.4 0.9 collective-permute-start.7
  43.4 0.7 sub.14
  44.0 7.2 %all-to-all-start = ((s32[16,1,64]{2,1,0:T(1,128)}), s32[16,1,64]{2,1,0:T(1,128)S(1)}, u32[]{:S(2)}, u32[]{:S(2)}) async-start(s32[16,1,64]{2,1,0:T(1,128)} %bitcast.10), calls=%async_computation | async-start | bytes 16384 | tf_op jit(solution)/shard_map/all_to_all | solution.py:251
  51.3 0.6 copy.29
  51.9 5.8 %all-to-all-done = s32[16,1,64]{2,1,0:T(1,128)S(1)} async-done(((s32[16,1,64]{2,1,0:T(1,128)}), s32[16,1,64]{2,1,0:T(1,128)S(1)}, u32[]{:S(2)}, u32[]{:S(2)}) %all-to-all-start) | async-done | bytes 4128 | tf_op jit(solution)/shard_map/all_to_all | solution.py:251
  57.7 0.6 broadcast.72
  58.3 0.7 reduce.9
  58.9 1.3 broadcast_in_dim_reshape.8.cells_col
  60.2 0.6 copy-done.19
  60.8 14.8 %shard_map.119 = (bf16[2048,256]{1,0:T(8,128)(2,1)}, f32[2048,128]{1,0:T(8,128)}, bf16[2048,512]{1,0:T(8,128)(2,1)}, f32[1024,128]{1,0:T(8,128)}) custom-call(bf16[32,64,256]{2,1,0:T(8,128)(2,1)} %get-tuple-element.17.x, bf16[2,64,256]{2,1,0:T(8,128)(2,1)} %copy-done.18, bf16[2,64,256]{2,1,0:T(8,128)(2,1)} %copy-done.17, bf16[36,2,256]{2,1,0:T(2,128)(2,1)} %copy-done.19, ...), custom_call_target="tpu_custom_call" | custom-call | flops 1099956224 | bytes 6592512 | tf_op jit(solution)/shard_map/pallas_call | solution.py:206
  75.6 1.5 collective-permute-start.8
  77.1 1.2 fusion.2
  78.3 3.5 %all-to-all-start.1 = ((bf16[16,64,128]{2,1,0:T(8,128)(2,1)}), bf16[16,64,128]{2,1,0:T(8,128)(2,1)S(1)}, u32[]{:S(2)}, u32[]{:S(2)}) async-start(bf16[16,64,128]{2,1,0:T(8,128)(2,1)} %bitcast.11), calls=%async_computation.1 | async-start | bytes 524288 | tf_op jit(solution)/shard_map/all_to_all | solution.py:248
  81.8 0.7 broadcast_in_dim_reshape.7.cells_row
  82.5 9.3 %all-to-all-done.1 = bf16[16,64,128]{2,1,0:T(8,128)(2,1)S(1)} async-done(((bf16[16,64,128]{2,1,0:T(8,128)(2,1)}), bf16[16,64,128]{2,1,0:T(8,128)(2,1)S(1)}, u32[]{:S(2)}, u32[]{:S(2)}) %all-to-all-start.1) | async-done | bytes 262176 | tf_op jit(solution)/shard_map/all_to_all | solution.py:248
  91.8 0.7 copy-done.1
  92.5 0.2 copy-done.2
  92.7 9.4 %shard_map.120 = (f32[2048,256]{1,0:T(8,128)}, bf16[32,64,256]{2,1,0:T(8,128)(2,1)}) custom-call(f32[1024,128]{1,0:T(8,128)} %get-tuple-element.18.mine, f32[1024,128]{1,0:T(8,128)} %copy-done.2, bf16[1024,128]{1,0:T(8,128)(2,1)} %bitcast.34, s32[1,1024]{1,0:T(1,128)} %broadcast_in_dim_reshape.7.cells_row, bf16[256,128]{1,0:T(8,128)(2,1)} %op.3, ...), custom_call_target="tpu_custom_call" | custom-call | flops 1073741824 | bytes 9246208 | tf_op jit(solution)/shard_map/pallas_call | solution.py:206
  102.1 0.9 fusion.22
  103.0 1.3 collective-permute-start.10
  104.3 1.0 fusion.21
  105.3 4.5 %collective-permute-start.9 = (bf16[2,64,256]{2,1,0:T(8,128)(2,1)S(1)}, bf16[2,64,256]{2,1,0:T(8,128)(2,1)S(1)}, u32[]{:S(2)}, u32[]{:S(2)}) collective-permute-start(bf16[2,64,256]{2,1,0:T(8,128)(2,1)S(1)} %get-tuple-element.36), channel_id=1, source_target_pairs={{0,8},{8,16},{16,24},{1,9},{9,17},{17,25},{2,10},{10,18},{18,26},{... | collective-permute-start | bytes 196616 | tf_op jit(solution)/shard_map/ppermute | solution.py:223
  109.9 1.8 %collective-permute-done.9.up = bf16[2,64,256]{2,1,0:T(8,128)(2,1)S(1)} collective-permute-done((bf16[2,64,256]{2,1,0:T(8,128)(2,1)S(1)}, bf16[2,64,256]{2,1,0:T(8,128)(2,1)S(1)}, u32[]{:S(2)}, u32[]{:S(2)}) %collective-permute-start.9) | collective-permute-done | bytes 65568 | tf_op jit(solution)/shard_map/ppermute | solution.py:223
  112.0 1.8 %collective-permute-start.12 = (bf16[36,2,256]{2,1,0:T(2,128)(2,1)S(1)}, bf16[36,2,256]{2,1,0:T(2,128)(2,1)S(1)}, u32[]{:S(2)}, u32[]{:S(2)}) collective-permute-start(bf16[36,2,256]{2,1,0:T(2,128)(2,1)S(1)} %pad_maximum_fusion.5), channel_id=1, source_target_pairs={{2,0},{4,2},{6,4},{0,6},{3,1},{5,3},{7,5},{1,7},{10,8},{12,10},{14... | collective-permute-start | bytes 110600 | tf_op jit(solution)/shard_map/ppermute | solution.py:228
  113.7 0.6 slice.188
  114.4 1.2 collective-permute-done.11.left
  115.6 0.6 copy-done.10
  116.2 12.6 %shard_map.121 = (f32[2048,256]{1,0:T(8,128)}, bf16[32,64,256]{2,1,0:T(8,128)(2,1)}) custom-call(bf16[32,64,256]{2,1,0:T(8,128)(2,1)} %get-tuple-element.22.dh, bf16[2,64,256]{2,1,0:T(8,128)(2,1)} %copy-done.7, bf16[2,64,256]{2,1,0:T(8,128)(2,1)} %copy-done.6, bf16[36,2,256]{2,1,0:T(2,128)(2,1)} %copy-done.10, bf16[36,2,256]{2,1,0:T(2,128)(2,1)} %copy-done.11, ...), custom_call_target="tpu_custom_call" | custom-call | flops 1099956224 | bytes 11241472 | tf_op jit(solution)/shard_map/pallas_call | solution.py:206
  128.8 0.9 fusion.20
  129.7 1.3 collective-permute-start.14
  131.0 1.0 fusion.19
  132.0 4.9 %collective-permute-start.13 = (bf16[2,64,256]{2,1,0:T(8,128)(2,1)S(1)}, bf16[2,64,256]{2,1,0:T(8,128)(2,1)S(1)}, u32[]{:S(2)}, u32[]{:S(2)}) collective-permute-start(bf16[2,64,256]{2,1,0:T(8,128)(2,1)S(1)} %get-tuple-element.32), channel_id=1, source_target_pairs={{0,8},{8,16},{16,24},{1,9},{9,17},{17,25},{2,10},{10,18},{18,26},{... | collective-permute-start | bytes 196616 | tf_op jit(solution)/shard_map/ppermute | solution.py:223
  137.0 1.8 %collective-permute-done.13.up = bf16[2,64,256]{2,1,0:T(8,128)(2,1)S(1)} collective-permute-done((bf16[2,64,256]{2,1,0:T(8,128)(2,1)S(1)}, bf16[2,64,256]{2,1,0:T(8,128)(2,1)S(1)}, u32[]{:S(2)}, u32[]{:S(2)}) %collective-permute-start.13) | collective-permute-done | bytes 65568 | tf_op jit(solution)/shard_map/ppermute | solution.py:223
  139.0 1.8 %collective-permute-start.16 = (bf16[36,2,256]{2,1,0:T(2,128)(2,1)S(1)}, bf16[36,2,256]{2,1,0:T(2,128)(2,1)S(1)}, u32[]{:S(2)}, u32[]{:S(2)}) collective-permute-start(bf16[36,2,256]{2,1,0:T(2,128)(2,1)S(1)} %pad_maximum_fusion.7), channel_id=1, source_target_pairs={{2,0},{4,2},{6,4},{0,6},{3,1},{5,3},{7,5},{1,7},{10,8},{12,10},{14... | collective-permute-start | bytes 110600 | tf_op jit(solution)/shard_map/ppermute | solution.py:228
  140.8 0.6 slice.197
  141.5 1.3 collective-permute-done.15.left
  142.8 0.6 copy-done.12
  143.4 9.7 %shard_map.122 = f32[32,64,256]{2,1,0:T(8,128)} custom-call(bf16[32,64,256]{2,1,0:T(8,128)(2,1)} %get-tuple-element.27.dh, bf16[2,64,256]{2,1,0:T(8,128)(2,1)} %copy-done.9, bf16[2,64,256]{2,1,0:T(8,128)(2,1)} %copy-done.8, bf16[36,2,256]{2,1,0:T(2,128)(2,1)} %copy-done.12, bf16[36,2,256]{2,1,0:T(2,128)(2,1)} %copy-done.13, f32[25,256]{1,0:T(8,128)} %bitcast.36, ...), custom_call_target="tpu_custom_call" | custom-call | flops 26214400 | bytes 7571456 | tf_op jit(solution)/shard_map/pallas_call | solution.py:206
  (71 shorter events, 0.9 us)
Async XLA Ops:
  0.0 77.1 %copy-start = (bf16[512,128]{1,0:T(8,128)(2,1)S(1)}, bf16[512,128]{1,0:T(8,128)(2,1)}, u32[]{:S(2)}) copy-start(bf16[512,128]{1,0:T(8,128)(2,1)} %param.21) | copy-start | bytes 393220
  0.0 14.1 %copy-start.3 = (bf16[2,512,256]{2,1,0:T(8,128)(2,1)S(1)}, bf16[2,512,256]{2,1,0:T(8,128)(2,1)}, u32[]{:S(2)}) copy-start(bf16[2,512,256]{2,1,0:T(8,128)(2,1)} %param.18) | copy-start | bytes 1572868
  0.0 17.5 %copy-start.14 = (f32[2,256]{1,0:T(2,128)S(1)}, f32[2,256]{1,0:T(2,128)}, u32[]{:S(2)}) copy-start(f32[2,256]{1,0:T(2,128)} %param.16) | copy-start | bytes 6148
  1.0 14.5 %collective-permute-start.1 = (bf16[2,64,256]{2,1,0:T(8,128)(2,1)S(1)}, bf16[2,64,256]{2,1,0:T(8,128)(2,1)S(1)}, u32[]{:S(2)}, u32[]{:S(2)}) collective-permute-start(bf16[2,64,256]{2,1,0:T(8,128)(2,1)S(1)} %get-tuple-element.43), channel_id=1, source_target_pairs={{8,0},{16,8},{24,16},{9,1},{17,9},{25,17},{10,2},{18,10},{26,18},{... | collective-permute-start | bytes 196616 | tf_op jit(solution)/shard_map/ppermute | solution.py:224
  2.3 13.2 %collective-permute-start = (bf16[2,64,256]{2,1,0:T(8,128)(2,1)S(1)}, bf16[2,64,256]{2,1,0:T(8,128)(2,1)S(1)}, u32[]{:S(2)}, u32[]{:S(2)}) collective-permute-start(bf16[2,64,256]{2,1,0:T(8,128)(2,1)S(1)} %get-tuple-element.44), channel_id=1, source_target_pairs={{0,8},{8,16},{16,24},{1,9},{9,17},{17,25},{2,10},{10,18},{18,26},{... | collective-permute-start | bytes 196616 | tf_op jit(solution)/shard_map/ppermute | solution.py:223
  15.4 3.7 %copy-start.15 = (bf16[2,64,256]{2,1,0:T(8,128)(2,1)}, bf16[2,64,256]{2,1,0:T(8,128)(2,1)S(1)}, u32[]{:S(2)}) copy-start(bf16[2,64,256]{2,1,0:T(8,128)(2,1)S(1)} %collective-permute-done.1.refs_2_) | copy-start | bytes 196612
  15.5 3.6 %copy-start.16 = (bf16[2,64,256]{2,1,0:T(8,128)(2,1)}, bf16[2,64,256]{2,1,0:T(8,128)(2,1)S(1)}, u32[]{:S(2)}) copy-start(bf16[2,64,256]{2,1,0:T(8,128)(2,1)S(1)} %collective-permute-done.refs_1_) | copy-start | bytes 196612
  15.6 3.4 %collective-permute-start.2 = (bf16[36,2,256]{2,1,0:T(2,128)(2,1)S(1)}, bf16[36,2,256]{2,1,0:T(2,128)(2,1)S(1)}, u32[]{:S(2)}, u32[]{:S(2)}) collective-permute-start(bf16[36,2,256]{2,1,0:T(2,128)(2,1)S(1)} %pad_maximum_fusion), channel_id=1, source_target_pairs={{0,2},{2,4},{4,6},{6,0},{1,3},{3,5},{5,7},{7,1},{8,10},{10,12},{12... | collective-permute-start | bytes 110600 | tf_op jit(solution)/shard_map/ppermute | solution.py:227
  15.7 3.4 %collective-permute-start.3 = (bf16[36,2,256]{2,1,0:T(2,128)(2,1)S(1)}, bf16[36,2,256]{2,1,0:T(2,128)(2,1)S(1)}, u32[]{:S(2)}, u32[]{:S(2)}) collective-permute-start(bf16[36,2,256]{2,1,0:T(2,128)(2,1)S(1)} %pad_maximum_fusion.1), channel_id=1, source_target_pairs={{2,0},{4,2},{6,4},{0,6},{3,1},{5,3},{7,5},{1,7},{10,8},{12,10},{14... | collective-permute-start | bytes 110600 | tf_op jit(solution)/shard_map/ppermute | solution.py:228
  19.0 0.6 copy-start.21
  19.1 0.6 copy-start.22
  32.6 6.9 %collective-permute-start.5 = (bf16[2,64,256]{2,1,0:T(8,128)(2,1)S(1)}, bf16[2,64,256]{2,1,0:T(8,128)(2,1)S(1)}, u32[]{:S(2)}, u32[]{:S(2)}) collective-permute-start(bf16[2,64,256]{2,1,0:T(8,128)(2,1)S(1)} %get-tuple-element.39), channel_id=1, source_target_pairs={{8,0},{16,8},{24,16},{9,1},{17,9},{25,17},{10,2},{18,10},{26,18},{... | collective-permute-start | bytes 196616 | tf_op jit(solution)/shard_map/ppermute | solution.py:224
  34.9 6.4 %collective-permute-start.4 = (bf16[2,64,256]{2,1,0:T(8,128)(2,1)S(1)}, bf16[2,64,256]{2,1,0:T(8,128)(2,1)S(1)}, u32[]{:S(2)}, u32[]{:S(2)}) collective-permute-start(bf16[2,64,256]{2,1,0:T(8,128)(2,1)S(1)} %get-tuple-element.40), channel_id=1, source_target_pairs={{0,8},{8,16},{16,24},{1,9},{9,17},{17,25},{2,10},{10,18},{18,26},{... | collective-permute-start | bytes 196616 | tf_op jit(solution)/shard_map/ppermute | solution.py:223
  39.5 20.7 %copy-start.17 = (bf16[2,64,256]{2,1,0:T(8,128)(2,1)}, bf16[2,64,256]{2,1,0:T(8,128)(2,1)S(1)}, u32[]{:S(2)}) copy-start(bf16[2,64,256]{2,1,0:T(8,128)(2,1)S(1)} %collective-permute-done.5.down) | copy-start | bytes 196612
  41.3 18.9 %copy-start.18 = (bf16[2,64,256]{2,1,0:T(8,128)(2,1)}, bf16[2,64,256]{2,1,0:T(8,128)(2,1)S(1)}, u32[]{:S(2)}) copy-start(bf16[2,64,256]{2,1,0:T(8,128)(2,1)S(1)} %collective-permute-done.4.up) | copy-start | bytes 196612
  41.4 18.8 %collective-permute-start.6 = (bf16[36,2,256]{2,1,0:T(2,128)(2,1)S(1)}, bf16[36,2,256]{2,1,0:T(2,128)(2,1)S(1)}, u32[]{:S(2)}, u32[]{:S(2)}) collective-permute-start(bf16[36,2,256]{2,1,0:T(2,128)(2,1)S(1)} %pad_maximum_fusion.2), channel_id=1, source_target_pairs={{0,2},{2,4},{4,6},{6,0},{1,3},{3,5},{5,7},{7,1},{8,10},{10,12},{12... | collective-permute-start | bytes 110600 | tf_op jit(solution)/shard_map/ppermute | solution.py:227
  42.4 17.7 %collective-permute-start.7 = (bf16[36,2,256]{2,1,0:T(2,128)(2,1)S(1)}, bf16[36,2,256]{2,1,0:T(2,128)(2,1)S(1)}, u32[]{:S(2)}, u32[]{:S(2)}) collective-permute-start(bf16[36,2,256]{2,1,0:T(2,128)(2,1)S(1)} %pad_maximum_fusion.3), channel_id=1, source_target_pairs={{2,0},{4,2},{6,4},{0,6},{3,1},{5,3},{7,5},{1,7},{10,8},{12,10},{14... | collective-permute-start | bytes 110600 | tf_op jit(solution)/shard_map/ppermute | solution.py:228
  44.0 13.7 %all-to-all-start = ((s32[16,1,64]{2,1,0:T(1,128)}), s32[16,1,64]{2,1,0:T(1,128)S(1)}, u32[]{:S(2)}, u32[]{:S(2)}) async-start(s32[16,1,64]{2,1,0:T(1,128)} %bitcast.10), calls=%async_computation | async-start | bytes 16384 | tf_op jit(solution)/shard_map/all_to_all | solution.py:251
  60.2 0.6 copy-start.19
  60.2 0.6 copy-start.20
  75.6 16.2 %collective-permute-start.8 = (f32[1024,128]{1,0:T(8,128)}, f32[1024,128]{1,0:T(8,128)S(1)}, u32[]{:S(2)}, u32[]{:S(2)}) collective-permute-start(f32[1024,128]{1,0:T(8,128)} %get-tuple-element.18.mine), channel_id=1, source_target_pairs={{0,1},{1,0},{2,3},{3,2},{4,5},{5,4},{6,7},{7,6},{8,9},{9,8},{10,11... | collective-permute-start | bytes 1572872 | tf_op jit(solution)/shard_map/ppermute | solution.py:311
  78.3 13.5 %all-to-all-start.1 = ((bf16[16,64,128]{2,1,0:T(8,128)(2,1)}), bf16[16,64,128]{2,1,0:T(8,128)(2,1)S(1)}, u32[]{:S(2)}, u32[]{:S(2)}) async-start(bf16[16,64,128]{2,1,0:T(8,128)(2,1)} %bitcast.11), calls=%async_computation.1 | async-start | bytes 524288 | tf_op jit(solution)/shard_map/all_to_all | solution.py:248
  91.8 0.7 copy-start.1
  91.8 0.9 copy-start.2
  92.7 21.0 %copy-start.5 = (f32[1,25,256]{2,1,0:T(8,128)S(1)}, f32[1,25,256]{2,1,0:T(8,128)}, u32[]{:S(2)}) copy-start(f32[1,25,256]{2,1,0:T(8,128)} %copy.29) | copy-start | bytes 76804
  103.0 6.9 %collective-permute-start.10 = (bf16[2,64,256]{2,1,0:T(8,128)(2,1)S(1)}, bf16[2,64,256]{2,1,0:T(8,128)(2,1)S(1)}, u32[]{:S(2)}, u32[]{:S(2)}) collective-permute-start(bf16[2,64,256]{2,1,0:T(8,128)(2,1)S(1)} %get-tuple-element.35), channel_id=1, source_target_pairs={{8,0},{16,8},{24,16},{9,1},{17,9},{25,17},{10,2},{18,10},{26,18},{... | collective-permute-start | bytes 196616 | tf_op jit(solution)/shard_map/ppermute | solution.py:224
  105.3 6.4 %collective-permute-start.9 = (bf16[2,64,256]{2,1,0:T(8,128)(2,1)S(1)}, bf16[2,64,256]{2,1,0:T(8,128)(2,1)S(1)}, u32[]{:S(2)}, u32[]{:S(2)}) collective-permute-start(bf16[2,64,256]{2,1,0:T(8,128)(2,1)S(1)} %get-tuple-element.36), channel_id=1, source_target_pairs={{0,8},{8,16},{16,24},{1,9},{9,17},{17,25},{2,10},{10,18},{18,26},{... | collective-permute-start | bytes 196616 | tf_op jit(solution)/shard_map/ppermute | solution.py:223
  109.9 5.7 %copy-start.6 = (bf16[2,64,256]{2,1,0:T(8,128)(2,1)}, bf16[2,64,256]{2,1,0:T(8,128)(2,1)S(1)}, u32[]{:S(2)}) copy-start(bf16[2,64,256]{2,1,0:T(8,128)(2,1)S(1)} %collective-permute-done.10.down) | copy-start | bytes 196612
  111.7 3.8 %copy-start.7 = (bf16[2,64,256]{2,1,0:T(8,128)(2,1)}, bf16[2,64,256]{2,1,0:T(8,128)(2,1)S(1)}, u32[]{:S(2)}) copy-start(bf16[2,64,256]{2,1,0:T(8,128)(2,1)S(1)} %collective-permute-done.9.up) | copy-start | bytes 196612
  111.8 3.8 %collective-permute-start.11 = (bf16[36,2,256]{2,1,0:T(2,128)(2,1)S(1)}, bf16[36,2,256]{2,1,0:T(2,128)(2,1)S(1)}, u32[]{:S(2)}, u32[]{:S(2)}) collective-permute-start(bf16[36,2,256]{2,1,0:T(2,128)(2,1)S(1)} %pad_maximum_fusion.4), channel_id=1, source_target_pairs={{0,2},{2,4},{4,6},{6,0},{1,3},{3,5},{5,7},{7,1},{8,10},{10,12},{12... | collective-permute-start | bytes 110600 | tf_op jit(solution)/shard_map/ppermute | solution.py:227
  112.0 3.6 %collective-permute-start.12 = (bf16[36,2,256]{2,1,0:T(2,128)(2,1)S(1)}, bf16[36,2,256]{2,1,0:T(2,128)(2,1)S(1)}, u32[]{:S(2)}, u32[]{:S(2)}) collective-permute-start(bf16[36,2,256]{2,1,0:T(2,128)(2,1)S(1)} %pad_maximum_fusion.5), channel_id=1, source_target_pairs={{2,0},{4,2},{6,4},{0,6},{3,1},{5,3},{7,5},{1,7},{10,8},{12,10},{14... | collective-permute-start | bytes 110600 | tf_op jit(solution)/shard_map/ppermute | solution.py:228
  115.6 0.6 copy-start.10
  115.6 0.6 copy-start.11
  116.2 24.6 %copy-start.4 = (f32[1,25,256]{2,1,0:T(8,128)S(1)}, f32[1,25,256]{2,1,0:T(8,128)}, u32[]{:S(2)}) copy-start(f32[1,25,256]{2,1,0:T(8,128)} %copy.28) | copy-start | bytes 76804
  129.7 7.3 %collective-permute-start.14 = (bf16[2,64,256]{2,1,0:T(8,128)(2,1)S(1)}, bf16[2,64,256]{2,1,0:T(8,128)(2,1)S(1)}, u32[]{:S(2)}, u32[]{:S(2)}) collective-permute-start(bf16[2,64,256]{2,1,0:T(8,128)(2,1)S(1)} %get-tuple-element.31), channel_id=1, source_target_pairs={{8,0},{16,8},{24,16},{9,1},{17,9},{25,17},{10,2},{18,10},{26,18},{... | collective-permute-start | bytes 196616 | tf_op jit(solution)/shard_map/ppermute | solution.py:224
  132.0 6.8 %collective-permute-start.13 = (bf16[2,64,256]{2,1,0:T(8,128)(2,1)S(1)}, bf16[2,64,256]{2,1,0:T(8,128)(2,1)S(1)}, u32[]{:S(2)}, u32[]{:S(2)}) collective-permute-start(bf16[2,64,256]{2,1,0:T(8,128)(2,1)S(1)} %get-tuple-element.32), channel_id=1, source_target_pairs={{0,8},{8,16},{16,24},{1,9},{9,17},{17,25},{2,10},{10,18},{18,26},{... | collective-permute-start | bytes 196616 | tf_op jit(solution)/shard_map/ppermute | solution.py:223
  137.0 5.8 %copy-start.8 = (bf16[2,64,256]{2,1,0:T(8,128)(2,1)}, bf16[2,64,256]{2,1,0:T(8,128)(2,1)S(1)}, u32[]{:S(2)}) copy-start(bf16[2,64,256]{2,1,0:T(8,128)(2,1)S(1)} %collective-permute-done.14.down) | copy-start | bytes 196612
  138.8 3.9 %copy-start.9 = (bf16[2,64,256]{2,1,0:T(8,128)(2,1)}, bf16[2,64,256]{2,1,0:T(8,128)(2,1)S(1)}, u32[]{:S(2)}) copy-start(bf16[2,64,256]{2,1,0:T(8,128)(2,1)S(1)} %collective-permute-done.13.up) | copy-start | bytes 196612
  138.9 3.8 %collective-permute-start.15 = (bf16[36,2,256]{2,1,0:T(2,128)(2,1)S(1)}, bf16[36,2,256]{2,1,0:T(2,128)(2,1)S(1)}, u32[]{:S(2)}, u32[]{:S(2)}) collective-permute-start(bf16[36,2,256]{2,1,0:T(2,128)(2,1)S(1)} %pad_maximum_fusion.6), channel_id=1, source_target_pairs={{0,2},{2,4},{4,6},{6,0},{1,3},{3,5},{5,7},{7,1},{8,10},{10,12},{12... | collective-permute-start | bytes 110600 | tf_op jit(solution)/shard_map/ppermute | solution.py:227
  139.0 3.7 %collective-permute-start.16 = (bf16[36,2,256]{2,1,0:T(2,128)(2,1)S(1)}, bf16[36,2,256]{2,1,0:T(2,128)(2,1)S(1)}, u32[]{:S(2)}, u32[]{:S(2)}) collective-permute-start(bf16[36,2,256]{2,1,0:T(2,128)(2,1)S(1)} %pad_maximum_fusion.7), channel_id=1, source_target_pairs={{2,0},{4,2},{6,4},{0,6},{3,1},{5,3},{7,5},{1,7},{10,8},{12,10},{14... | collective-permute-start | bytes 110600 | tf_op jit(solution)/shard_map/ppermute | solution.py:228
  142.7 0.6 copy-start.12
  142.7 0.6 copy-start.13

commit v2 on v0

v2 whole, which is shorter than its diff:
```python
import functools

import jax
import jax.numpy as jnp
from jax import lax
from jax.experimental import pallas as pl
from jax.experimental.pallas import tpu as pltpu
from jax.sharding import PartitionSpec as P

SQRT_TWO_OVER_PI = 0.7978845608
CUBIC = 0.044715
EPSILON = 1e-06
LANES = 128
ROWS = 8
VMEM_BYTES = 56 * 1024 * 1024


def dot(a, b):
    return jnp.dot(a, b, preferred_element_type=jnp.float32)


def dot_t(a, b):
    return lax.dot_general(a, b, (((1,), (1,)), ((), ())), preferred_element_type=jnp.float32)


DIRECTIONS = ((-1, 0), (1, 0), (0, -1), (0, 1), (-1, -1), (-1, 1), (1, -1), (1, 1))
MESH = pl.DeviceIdType.MESH


def conv_rows(xs, taps, out, r0, flip):
    width, channels = xs.shape[2], xs.shape[3]

    def column(step, carry):
        c0 = pl.multiple_of(step * 8, 8)
        for part in range(channels // LANES):
            lanes = slice(part * LANES, (part + 1) * LANES)
            acc = None
            for j in range(5):
                xj = xs[j, pl.ds(r0, ROWS + 4), pl.ds(c0, 8), lanes]
                for i in range(5):
                    at = 24 - (5 * i + j) if flip else 5 * i + j
                    term = taps[at : at + 1, lanes][None] * xj[i : i + ROWS]
                    acc = term if acc is None else acc + term
            out[:, pl.ds(c0, 8), lanes] = acc
        return carry

    lax.fori_loop(0, width // 8, column, 0)


def forward_block(h, x, gain, w_in, w_out):
    s = lax.rsqrt(jnp.mean(h * h, axis=1, keepdims=True) + EPSILON)
    n = (h * s * gain).astype(jnp.bfloat16)
    z = dot(n, w_in)
    zz = z * z
    inner = jnp.tanh(z * (SQRT_TWO_OVER_PI + (SQRT_TWO_OVER_PI * CUBIC) * zz))
    half = 0.5 + 0.5 * inner
    t = (z * half).astype(jnp.bfloat16)
    slope = half + (z * (0.5 - 0.5 * inner * inner)) * (
        SQRT_TWO_OVER_PI + (SQRT_TWO_OVER_PI * 3.0 * CUBIC) * zz
    )
    mixed = dot(t, w_out)
    return s, n, slope.astype(jnp.bfloat16), (x.astype(jnp.float32) + mixed).astype(jnp.bfloat16)


def backward_block(g, n, s, slope, gain, w_in, w_out):
    u = dot_t(g.astype(jnp.bfloat16), w_out)
    dz = (u * slope.astype(jnp.float32)).astype(jnp.bfloat16)
    dn = dot_t(dz, w_in)
    nf = n.astype(jnp.float32)
    m = jnp.mean(dn * nf, axis=1, keepdims=True)
    return (s * (gain * dn - (nf * (1.0 / gain)) * m)).astype(jnp.bfloat16)


def kernel(
    mesh_shape,
    x,
    background,
    prior_precision,
    taps,
    gains,
    w_in,
    w_out,
    op,
    precision,
    obs_values,
    owner,
    cell,
    out,
    middle,
    last,
    cotangent,
    grad,
    n_keep,
    s_keep,
    slope_keep,
    xp,
    xs,
    hb,
    stage_side,
    stage_corner,
    got_edge,
    got_side,
    got_corner,
    outbox,
    inbox,
    mine,
    other,
    halo_send,
    halo_recv,
    box_send,
    box_recv,
    ens_send,
    ens_recv,
):
    f32, bf16 = jnp.float32, jnp.bfloat16
    lats, lons, members = mesh_shape
    height, width, channels = x.shape
    lat, lon, ens = lax.axis_index("lat"), lax.axis_index("lon"), lax.axis_index("ens")
    grid = lats * lons
    me = lat * lons + lon
    slots = inbox.shape[0]
    capacity = slots // grid
    partner = {"lat": lat, "lon": lon, "ens": 1 - ens}
    cells = ROWS * width

    def peer(k):
        to = lax.rem(me + k, grid)
        return {"lat": to // lons, "lon": lax.rem(to, lons), "ens": ens}

    barrier = pltpu.get_barrier_semaphore()

    def greet(k, carry):
        pl.semaphore_signal(barrier, inc=1, device_id=peer(k), device_id_type=MESH)
        return carry

    lax.fori_loop(1, grid, greet, 0)
    pl.semaphore_signal(barrier, inc=1, device_id=partner, device_id_type=MESH)
    pl.semaphore_wait(barrier, grid)

    def send(step, field):
        def fill(k, carry):
            r = k * 4
            xp[pl.ds(r + 2, 4), 8 : 8 + width] = field[pl.ds(r, 4)].astype(f32)
            return carry

        lax.fori_loop(0, height // 4, fill, 0)
        for side, first in ((0, 8), (1, 6 + width)):
            for c in range(2):
                stage_side[step, side, c * height : (c + 1) * height] = xp[2 : 2 + height, first + c, :]
        for k, (down, east) in enumerate(DIRECTIONS[4:]):
            r0 = 2 if down < 0 else height
            c0 = 8 if east < 0 else 6 + width
            for r in range(2):
                stage_corner[step, k, 4 * r : 4 * r + 2] = xp[r0 + r, c0 : c0 + 2, :]
        copies = []
        for d, (down, east) in enumerate(DIRECTIONS):
            if d < 2:
                source = field.at[0:2] if down < 0 else field.at[height - 2 : height]
                target = got_edge.at[step, d]
            elif d < 4:
                source, target = stage_side.at[step, d - 2], got_side.at[step, d - 2]
            else:
                source, target = stage_corner.at[step, d - 4], got_corner.at[step, d - 4]
            copy = pltpu.make_async_remote_copy(
                src_ref=source,
                dst_ref=target,
                send_sem=halo_send.at[step, d],
                recv_sem=halo_recv.at[step, d],
                device_id={
                    "lat": lax.rem(lat + down + lats, lats),
                    "lon": lax.rem(lon + east + lons, lons),
                    "ens": ens,
                },
                device_id_type=MESH,
            )
            copy.start()
            copies.append(copy)
        return copies

    def receive(step, copies):
        for copy in copies:
            copy.wait()
        above = (lat > 0).astype(f32)
        below = (lat < lats - 1).astype(f32)
        xp[height + 2 : height + 4, 8 : 8 + width] = got_edge[step, 0].astype(f32) * below
        xp[0:2, 8 : 8 + width] = got_edge[step, 1].astype(f32) * above
        for side, first in ((0, 8 + width), (1, 6)):
            for c in range(2):
                xp[2 : 2 + height, first + c, :] = got_side[step, side, c * height : (c + 1) * height]
        for k, (down, east) in enumerate(DIRECTIONS[4:]):
            r0, keep = (height + 2, below) if down < 0 else (0, above)
            c0 = 8 + width if east < 0 else 6
            for r in range(2):
                xp[r0 + r, c0 : c0 + 2, :] = got_corner[step, k, 4 * r : 4 * r + 2] * keep

        def shift(k, carry):
            r = k * 4
            for j in range(5):
                xs[j, pl.ds(r, 4)] = xp[pl.ds(r, 4), 6 + j : 6 + j + width]
            return carry

        lax.fori_loop(0, (height + 4) // 4, shift, 0)

    def flat_rows(k):
        return pl.ds(pl.multiple_of(k * cells, cells), cells)

    def forward(layer, field, new_field):
        def block(k, carry):
            rows = pl.ds(k * ROWS, ROWS)
            conv_rows(xs, taps.at[layer], hb, k * ROWS, False)
            s, n, slope, new = forward_block(
                hb[...].reshape(cells, channels),
                field[rows].reshape(cells, channels),
                gains[layer : layer + 1],
                w_in[layer],
                w_out[layer],
            )
            new_field[rows] = new.reshape(ROWS, width, channels)
            n_keep[layer, flat_rows(k)] = n
            s_keep[layer, flat_rows(k)] = jnp.broadcast_to(s, (cells, LANES))
            slope_keep[layer, flat_rows(k)] = slope
            return carry

        lax.fori_loop(0, height // ROWS, block, 0)

    def backward(layer, k, g, slot):
        flat = flat_rows(k)
        dh = backward_block(
            g,
            n_keep[layer, flat],
            s_keep[layer, flat][:, 0:1],
            slope_keep[layer, flat],
            gains[layer : layer + 1],
            w_in[layer],
            w_out[layer],
        )
        cotangent[slot, pl.ds(k * ROWS, ROWS)] = dh.reshape(ROWS, width, channels)

    copies = send(0, x)

    count, obs_channels = obs_values.shape
    hits = owner[...] == lax.broadcasted_iota(jnp.int32, (count, LANES), 1)
    hits = hits.astype(f32)
    order = lax.broadcasted_iota(jnp.int32, (count, count), 1)
    place = lax.broadcasted_iota(jnp.int32, (count, count), 0)
    earlier = dot((order < place).astype(f32).astype(bf16), hits.astype(bf16))
    rank = jnp.sum(hits * earlier, axis=1, keepdims=True).astype(jnp.int32)
    slot = owner[...] * capacity + rank
    hot = (lax.broadcasted_iota(jnp.int32, (count, slots), 1) == slot).astype(f32).astype(bf16)
    lane = lax.broadcasted_iota(jnp.int32, (count, LANES), 1)
    parts = jnp.where(lane == 0, cell[...] // 64, jnp.where(lane == 1, cell[...] % 64, jnp.where(lane == 2, 1, 0)))
    content = jnp.concatenate([obs_values[...], parts.astype(f32).astype(bf16)], axis=1)
    outbox[...] = lax.dot_general(
        hot, content, (((0,), (0,)), ((), ())), preferred_element_type=f32
    ).astype(outbox.dtype)

    def box(k):
        to = lax.rem(me + k, grid)
        return pltpu.make_async_remote_copy(
            src_ref=outbox.at[pl.ds(pl.multiple_of(to * capacity, capacity), capacity)],
            dst_ref=inbox.at[pl.ds(pl.multiple_of(me * capacity, capacity), capacity)],
            send_sem=box_send.at[k],
            recv_sem=box_recv.at[k],
            device_id=peer(k),
            device_id_type=MESH,
        )

    def post(k, carry):
        box(k).start()
        return carry

    lax.fori_loop(1, grid, post, 0)
    own = pl.ds(pl.multiple_of(me * capacity, capacity), capacity)
    inbox[own] = outbox[own]

    receive(0, copies)
    forward(0, x, middle)
    copies = send(1, middle)
    receive(1, copies)
    forward(1, middle, last)

    def collect(k, carry):
        box(k).wait()
        return carry

    lax.fori_loop(1, grid, collect, 0)
    chunk = slots // 4
    state = last[...].reshape(height * width, channels)
    lane8 = lax.broadcasted_iota(jnp.int32, (LANES, LANES), 1)
    pick = jnp.where(lane8 == 0, 64.0, jnp.where(lane8 < 3, 1.0, 0.0)).astype(bf16)
    exchanges = []
    for k in range(4):
        at = slice(k * chunk, (k + 1) * chunk)
        where_from = dot_t(inbox[at, obs_channels:].astype(bf16), pick)[:, 0:1].astype(jnp.int32) - 1
        places = lax.broadcasted_iota(jnp.int32, (chunk, height * width), 1)
        chosen = (places == where_from).astype(f32).astype(bf16)
        picked = dot(chosen, state).astype(bf16)
        mine[at] = dot(picked, op[...]).astype(bf16)
        copy = pltpu.make_async_remote_copy(
            src_ref=mine.at[at],
            dst_ref=other.at[at],
            send_sem=ens_send.at[k],
            recv_sem=ens_recv.at[k],
            device_id=partner,
            device_id_type=MESH,
        )
        copy.start()
        exchanges.append(copy)
    cells_row = dot_t(pick[0:16], inbox[:, obs_channels:].astype(bf16))[0:1].astype(jnp.int32) - 1
    for copy in exchanges:
        copy.wait()
    mean_pred = (mine[...].astype(f32) + other[...].astype(f32)) * (1.0 / members)
    misfit = mean_pred - inbox[:, 0:obs_channels].astype(f32)
    adj = (precision[...] * misfit * (1.0 / members)).astype(bf16)

    def spread(k, carry):
        places = lax.broadcasted_iota(jnp.int32, (cells, slots), 0) + k * cells
        chosen = (places == cells_row).astype(f32).astype(bf16)
        total = dot(chosen, adj)
        high = total.astype(bf16)
        low = (total - high.astype(f32)).astype(bf16)
        g = dot_t(high, op[...]) + dot_t(low, op[...])
        grad[flat_rows(k)] = g
        backward(1, k, g, 0)
        return carry

    lax.fori_loop(0, height // ROWS, spread, 0)
    copies = send(2, cotangent.at[0])
    receive(2, copies)

    def inner(k, carry):
        conv_rows(xs, taps.at[1], hb, k * ROWS, True)
        g = grad[flat_rows(k)] + hb[...].reshape(cells, channels)
        grad[flat_rows(k)] = g
        backward(0, k, g, 1)
        return carry

    lax.fori_loop(0, height // ROWS, inner, 0)
    copies = send(3, cotangent.at[1])
    receive(3, copies)

    def outer(k, carry):
        rows = pl.ds(k * ROWS, ROWS)
        conv_rows(xs, taps.at[0], hb, k * ROWS, True)
        diff = x[rows].astype(f32) - background[rows].astype(f32)
        prior = prior_precision[...] * diff.reshape(cells, channels)
        total = prior + (grad[flat_rows(k)] + hb[...].reshape(cells, channels))
        out[rows] = total.reshape(ROWS, width, channels)
        return carry

    lax.fori_loop(0, height // ROWS, outer, 0)


def per_device(
    mesh_shape,
    initial_state,
    background,
    background_precision,
    kernel_taps,
    norm_gains,
    weight_in,
    weight_out,
    obs_operator,
    obs_precision,
    obs_values,
    obs_owner,
    obs_cell,
):
    f32, bf16 = jnp.float32, jnp.bfloat16
    height, width, channels = initial_state.shape[1:]
    hidden = weight_in.shape[2]
    cells = height * width
    obs_channels = obs_values.shape[1]
    grid = mesh_shape[0] * mesh_shape[1]
    capacity = 2 * obs_values.shape[0] // grid
    slots = grid * capacity
    box_type = bf16 if capacity % 16 == 0 else f32
    whole = pl.BlockSpec(memory_space=pltpu.VMEM)
    args = (
        initial_state[0],
        background[0],
        background_precision[None, :],
        kernel_taps,
        norm_gains,
        weight_in,
        weight_out,
        obs_operator,
        obs_precision[None, :],
        obs_values,
        obs_owner,
        obs_cell[:, None],
    )
    out = pl.pallas_call(
        functools.partial(kernel, mesh_shape),
        out_shape=jax.ShapeDtypeStruct((height, width, channels), f32),
        in_specs=[whole] * len(args),
        out_specs=whole,
        scratch_shapes=[
            pltpu.VMEM((height, width, channels), bf16),
            pltpu.VMEM((height, width, channels), bf16),
            pltpu.VMEM((2, height, width, channels), bf16),
            pltpu.VMEM((cells, channels), f32),
            pltpu.VMEM((2, cells, channels), bf16),
            pltpu.VMEM((2, cells, LANES), f32),
            pltpu.VMEM((2, cells, hidden), bf16),
            pltpu.VMEM((height + 4, width + 16, channels), f32),
            pltpu.VMEM((5, height + 4, width, channels), f32),
            pltpu.VMEM((ROWS, width, channels), f32),
            pltpu.VMEM((4, 2, 2 * height, channels), f32),
            pltpu.VMEM((4, 4, 8, channels), f32),
            pltpu.VMEM((4, 2, 2, width, channels), bf16),
            pltpu.VMEM((4, 2, 2 * height, channels), f32),
            pltpu.VMEM((4, 4, 8, channels), f32),
            pltpu.VMEM((slots, obs_channels + LANES), box_type),
            pltpu.VMEM((slots, obs_channels + LANES), box_type),
            pltpu.VMEM((slots, obs_channels), bf16),
            pltpu.VMEM((slots, obs_channels), bf16),
            pltpu.SemaphoreType.DMA((4, 8)),
            pltpu.SemaphoreType.DMA((4, 8)),
            pltpu.SemaphoreType.DMA((grid,)),
            pltpu.SemaphoreType.DMA((grid,)),
            pltpu.SemaphoreType.DMA((4,)),
            pltpu.SemaphoreType.DMA((4,)),
        ],
        compiler_params=pltpu.CompilerParams(
            vmem_limit_bytes=VMEM_BYTES, collective_id=0, has_side_effects=True
        ),
    )(*args)
    return out[None]


def solution(mesh):
    mesh_shape = (mesh.shape["lat"], mesh.shape["lon"], mesh.shape["ens"])
    in_specs = (
        P("ens", "lat", "lon", None),
        P("ens", "lat", "lon", None),
        P(),
        P(),
        P(),
        P(),
        P(),
        P(),
        P(),
        P(("lat", "lon"), None),
        P(("lat", "lon"), None),
        P(("lat", "lon")),
    )
    out_specs = P("ens", "lat", "lon", None)
    return jax.shard_map(
        functools.partial(per_device, mesh_shape), mesh=mesh, in_specs=in_specs, out_specs=out_specs, check_vma=False
    )
```

time: 191 us -> 91.9 us (0.48)
  Pallas kernels: 0 us -> 84 us
  other arithmetic: 57.8 us -> 0 us
  waiting for transfers between devices: 37.9 us -> 0 us
  starting transfers between devices: 33.1 us -> 0 us
  matrix products: 26.7 us -> 0 us
  between operations: 14.8 us -> 0.01 us
  local copies, waits for them, and re-layouts: 19.2 us -> 7.64 us
    pallas_call x0 -> x1, Pallas kernels: none -> 84 us  [per_device(): pl.pallas_call(functools.partial(kernel, mesh_shape), out_shape=jax.Shape...]
    dot_general x8 -> x0, matrix products: 26.7 us -> none  [the longest x2 14.9 us: layer_back(): jnp.dot(hidden_grad, layer_in.T, preferred_element_type=jnp.float32)]
    ppermute x16 -> x0, starting transfers between devices: 24 us -> none  [the longest x8 15.4 us: extended(): lax.ppermute(lax.slice_in_dim(block, 0, width, axis=dim), axis, backward)]
    ppermute x16 -> x0, waiting for transfers between devices: 16.6 us -> none  [the longest x8 13.9 us: extended(): lax.ppermute(lax.slice_in_dim(block, block.shape[dim] - width, None, axis...]
    convert_element_type x6 -> x0, other arithmetic: 15.9 us -> none  [the longest x1 8.79 us: layer_back(): upstream.reshape(-1, channels).astype(jnp.bfloat16)]
    reduce_sum x3 -> x0, other arithmetic: 15.7 us -> none  [the longest x2 14.9 us: layer_front(): jnp.mean(flat_conv * flat_conv, axis=1, keepdims=True) + EPSILON]
    psum x1 -> x0, waiting for transfers between devices: 11.3 us -> none  [per_device(): ensemble_sum = lax.psum(predicted, 'ens')]
    all_to_all x2 -> x0, waiting for transfers between devices: 9.98 us -> none  [the longest x1 9.98 us: per_device(): lax.all_to_all(send_values.reshape(grid_count, capacity, obs_channels), (...]
  transfers between devices with their start and end apart: 19 -> 0, of which waited for: 11 -> 0; matrix products, arithmetic and copies ran while one was open for 9% -> 0% of each run, Pallas kernels for 0% -> 0%
where the time goes in v2:
time: 91.9 us; the launch traced here: 91.6 us
  Pallas kernels  84 us (91%)
  local copies, waits for them, and re-layouts  7.64 us (8%)
    pallas_call x1, Pallas kernels, per_device(): pl.pallas_call(functools.partial(kernel, mesh_shape), out_shape=jax.Shape...  84 us
    unnamed x3, local copies, waits for them, and re-layouts  6.09 us

profile of v2, /device:TPU:0, one launch (start us, length us, event | category | flops | bytes accessed | tf_op | source)
XLA Modules:
  0.0 91.6 jit_solution(12615382669739409603)
XLA Ops:
  0.0 1.4 %copy.15.taps = f32[2,25,256]{2,1,0:T(8,128)} copy(f32[2,25,256]{2,0,1:T(2,128)} %param.15) | data formatting | bytes 102400 | tf_op args[3]
  1.4 1.5 %copy.16.owner = s32[512,1]{1,0:T(8,128)} copy(s32[512,1]{0,1:T(1,128)} %param.22) | data formatting | bytes 4096 | tf_op args[10]
  3.0 1.6 %copy.17.cell = s32[512,1]{1,0:T(8,128)} copy(s32[512,1]{0,1:T(1,128)} %bitcast.9) | data formatting | bytes 4096 | tf_op jit(solution)/shard_map/broadcast_in_dim | solution.py:391
  4.5 84.0 %shard_map.118 = f32[32,64,256]{2,1,0:T(8,128)} custom-call(bf16[32,64,256]{2,1,0:T(8,128)(2,1)} %bitcast.7, bf16[32,64,256]{2,1,0:T(8,128)(2,1)} %bitcast.8, f32[1,256]{1,0:T(1,128)} %bitcast.10, f32[2,25,256]{2,1,0:T(8,128)} %copy.15.taps, f32[2,256]{1,0:T(2,128)} %gains.1, bf16[2,256,512]{2,1,0:T(8,128)(2,1)} %w_in.1, bf16[2,512,256]{2,1,0:T(8,128)(2,1)} %w_out.1, ...), custom_call_target="tpu_custom_call" | custom-call | tf_op jit(solution)/shard_map/pallas_call | solution.py:393
  88.5 3.1 %copy.19 = f32[1,32,64,256]{3,2,1,0:T(8,128)} copy(f32[1,32,64,256]{3,2,1,0:T(8,128)} %bitcast.6) | data formatting | bytes 4194304

commit v3 on v2

--- a/solution.py
+++ b/solution.py
@@ -44,7 +44,7 @@
             out[:, pl.ds(c0, 8), lanes] = acc
         return carry
 
-    lax.fori_loop(0, width // 8, column, 0)
+    lax.fori_loop(0, width // 8, column, 0, unroll=2)
 
 
 def forward_block(h, x, gain, w_in, w_out):
@@ -135,9 +135,8 @@
 
     lax.fori_loop(1, grid, greet, 0)
     pl.semaphore_signal(barrier, inc=1, device_id=partner, device_id_type=MESH)
-    pl.semaphore_wait(barrier, grid)
-
-    def send(step, field):
+
+    def prepare(step, field):
         def fill(k, carry):
             r = k * 4
             xp[pl.ds(r + 2, 4), 8 : 8 + width] = field[pl.ds(r, 4)].astype(f32)
@@ -152,6 +151,8 @@
             c0 = 8 if east < 0 else 6 + width
             for r in range(2):
                 stage_corner[step, k, 4 * r : 4 * r + 2] = xp[r0 + r, c0 : c0 + 2, :]
+
+    def launch(step, field):
         copies = []
         for d, (down, east) in enumerate(DIRECTIONS):
             if d < 2:
@@ -175,7 +176,19 @@
             )
             copy.start()
             copies.append(copy)
+
+        def shift(k, carry):
+            r = k * 4 + 2
+            for j in range(5):
+                xs[j, pl.ds(r, 4)] = xp[pl.ds(r, 4), 6 + j : 6 + j + width]
+            return carry
+
+        lax.fori_loop(0, height // 4, shift, 0)
         return copies
+
+    def send(step, field):
+        prepare(step, field)
+        return launch(step, field)
 
     def receive(step, copies):
         for copy in copies:
@@ -193,13 +206,19 @@
             for r in range(2):
                 xp[r0 + r, c0 : c0 + 2, :] = got_corner[step, k, 4 * r : 4 * r + 2] * keep
 
+        for r in (0, height + 2):
+            for j in range(5):
+                xs[j, r : r + 2] = xp[r : r + 2, 6 + j : 6 + j + width]
+
         def shift(k, carry):
-            r = k * 4
-            for j in range(5):
-                xs[j, pl.ds(r, 4)] = xp[pl.ds(r, 4), 6 + j : 6 + j + width]
+            rows = pl.ds(k * 8 + 2, 8)
+            for j in (0, 1):
+                xs[j, rows, 0:8] = xp[rows, 6 + j : 14 + j]
+            for j in (3, 4):
+                xs[j, rows, width - 8 : width] = xp[rows, width - 2 + j : width + 6 + j]
             return carry
 
-        lax.fori_loop(0, (height + 4) // 4, shift, 0)
+        lax.fori_loop(0, height // 8, shift, 0)
 
     def flat_rows(k):
         return pl.ds(pl.multiple_of(k * cells, cells), cells)
@@ -236,7 +255,7 @@
         )
         cotangent[slot, pl.ds(k * ROWS, ROWS)] = dh.reshape(ROWS, width, channels)
 
-    copies = send(0, x)
+    prepare(0, x)
 
     count, obs_channels = obs_values.shape
     hits = owner[...] == lax.broadcasted_iota(jnp.int32, (count, LANES), 1)
@@ -253,6 +272,9 @@
     outbox[...] = lax.dot_general(
         hot, content, (((0,), (0,)), ((), ())), preferred_element_type=f32
     ).astype(outbox.dtype)
+
+    pl.semaphore_wait(barrier, grid)
+    copies = launch(0, x)
 
     def box(k):
         to = lax.rem(me + k, grid)

time: 91.9 us -> 87.1 us (0.948)
  Pallas kernels: 84 us -> 79.2 us
    pallas_call x1, Pallas kernels: 84 us -> 79.2 us  [per_device(): pl.pallas_call(functools.partial(kernel, mesh_shape), out_shape=jax.Shape...]
where the time goes in v3:
time: 87.1 us; the launch traced here: 86.9 us
  Pallas kernels  79.2 us (91%)
  local copies, waits for them, and re-layouts  7.64 us (9%)
    pallas_call x1, Pallas kernels, per_device(): pl.pallas_call(functools.partial(kernel, mesh_shape), out_shape=jax.Shape...  79.2 us
    unnamed x3, local copies, waits for them, and re-layouts  6.09 us

profile of v3, /device:TPU:0, one launch (start us, length us, event | category | flops | bytes accessed | tf_op | source)
XLA Modules:
  0.0 86.9 jit_solution(12444933358056584990)
XLA Ops:
  0.0 1.4 %copy.15.taps = f32[2,25,256]{2,1,0:T(8,128)} copy(f32[2,25,256]{2,0,1:T(2,128)} %param.15) | data formatting | bytes 102400 | tf_op args[3]
  1.4 1.5 %copy.16.owner = s32[512,1]{1,0:T(8,128)} copy(s32[512,1]{0,1:T(1,128)} %param.22) | data formatting | bytes 4096 | tf_op args[10]
  3.0 1.6 %copy.17.cell = s32[512,1]{1,0:T(8,128)} copy(s32[512,1]{0,1:T(1,128)} %bitcast.9) | data formatting | bytes 4096 | tf_op jit(solution)/shard_map/broadcast_in_dim | solution.py:413
  4.5 79.2 %shard_map.118 = f32[32,64,256]{2,1,0:T(8,128)} custom-call(bf16[32,64,256]{2,1,0:T(8,128)(2,1)} %bitcast.7, bf16[32,64,256]{2,1,0:T(8,128)(2,1)} %bitcast.8, f32[1,256]{1,0:T(1,128)} %bitcast.10, f32[2,25,256]{2,1,0:T(8,128)} %copy.15.taps, f32[2,256]{1,0:T(2,128)} %gains.1, bf16[2,256,512]{2,1,0:T(8,128)(2,1)} %w_in.1, bf16[2,512,256]{2,1,0:T(8,128)(2,1)} %w_out.1, ...), custom_call_target="tpu_custom_call" | custom-call | tf_op jit(solution)/shard_map/pallas_call | solution.py:415
  83.7 3.1 %copy.19 = f32[1,32,64,256]{3,2,1,0:T(8,128)} copy(f32[1,32,64,256]{3,2,1,0:T(8,128)} %bitcast.6) | data formatting | bytes 4194304

commit v4 on v3

--- a/solution.py
+++ b/solution.py
@@ -76,7 +76,7 @@
     x,
     background,
     prior_precision,
-    taps,
+    tap_rows,
     gains,
     w_in,
     w_out,
@@ -111,6 +111,7 @@
     box_recv,
     ens_send,
     ens_recv,
+    taps,
 ):
     f32, bf16 = jnp.float32, jnp.bfloat16
     lats, lons, members = mesh_shape
@@ -256,22 +257,22 @@
         cotangent[slot, pl.ds(k * ROWS, ROWS)] = dh.reshape(ROWS, width, channels)
 
     prepare(0, x)
+    for t in range(tap_rows.shape[0]):
+        for layer in range(2):
+            taps[layer, t : t + 1] = tap_rows[t, layer : layer + 1]
 
     count, obs_channels = obs_values.shape
-    hits = owner[...] == lax.broadcasted_iota(jnp.int32, (count, LANES), 1)
-    hits = hits.astype(f32)
-    order = lax.broadcasted_iota(jnp.int32, (count, count), 1)
-    place = lax.broadcasted_iota(jnp.int32, (count, count), 0)
-    earlier = dot((order < place).astype(f32).astype(bf16), hits.astype(bf16))
-    rank = jnp.sum(hits * earlier, axis=1, keepdims=True).astype(jnp.int32)
+    hits = (owner[...] == lax.broadcasted_iota(jnp.int32, (LANES, count), 0)).astype(f32)
+    order = lax.broadcasted_iota(jnp.int32, (count, count), 0)
+    place = lax.broadcasted_iota(jnp.int32, (count, count), 1)
+    earlier = dot(hits.astype(bf16), (order < place).astype(f32).astype(bf16))
+    rank = jnp.sum(hits * earlier, axis=0, keepdims=True).astype(jnp.int32)
     slot = owner[...] * capacity + rank
-    hot = (lax.broadcasted_iota(jnp.int32, (count, slots), 1) == slot).astype(f32).astype(bf16)
-    lane = lax.broadcasted_iota(jnp.int32, (count, LANES), 1)
-    parts = jnp.where(lane == 0, cell[...] // 64, jnp.where(lane == 1, cell[...] % 64, jnp.where(lane == 2, 1, 0)))
-    content = jnp.concatenate([obs_values[...], parts.astype(f32).astype(bf16)], axis=1)
-    outbox[...] = lax.dot_general(
-        hot, content, (((0,), (0,)), ((), ())), preferred_element_type=f32
-    ).astype(outbox.dtype)
+    hot = (lax.broadcasted_iota(jnp.int32, (slots, count), 0) == slot).astype(f32).astype(bf16)
+    line = lax.broadcasted_iota(jnp.int32, (LANES, count), 0)
+    parts = jnp.where(line == 0, cell[...] // 64, jnp.where(line == 1, cell[...] % 64, jnp.where(line == 2, 1, 0)))
+    outbox[:, 0:obs_channels] = dot(hot, obs_values[...]).astype(outbox.dtype)
+    outbox[:, obs_channels:] = dot_t(hot, parts.astype(f32).astype(bf16)).astype(outbox.dtype)
 
     pl.semaphore_wait(barrier, grid)
     copies = launch(0, x)
@@ -402,15 +403,15 @@
         initial_state[0],
         background[0],
         background_precision[None, :],
-        kernel_taps,
+        jnp.swapaxes(kernel_taps, 0, 1),
         norm_gains,
         weight_in,
         weight_out,
         obs_operator,
         obs_precision[None, :],
         obs_values,
-        obs_owner,
-        obs_cell[:, None],
+        obs_owner.reshape(1, -1),
+        obs_cell[None, :],
     )
     out = pl.pallas_call(
         functools.partial(kernel, mesh_shape),
@@ -443,6 +444,7 @@
             pltpu.SemaphoreType.DMA((grid,)),
             pltpu.SemaphoreType.DMA((4,)),
             pltpu.SemaphoreType.DMA((4,)),
+            pltpu.VMEM(kernel_taps.shape, f32),
         ],
         compiler_params=pltpu.CompilerParams(
             vmem_limit_bytes=VMEM_BYTES, collective_id=0, has_side_effects=True

time: 87.1 us -> 82.5 us (0.947)
  local copies, waits for them, and re-layouts: 7.64 us -> 3.13 us
    unnamed x3 -> x1, local copies, waits for them, and re-layouts: 6.09 us -> 3.13 us
    broadcast_in_dim x1 -> x0, local copies, waits for them, and re-layouts: 1.56 us -> none  [per_device(): obs_cell[:, None]]
where the time goes in v4:
time: 82.5 us; the launch traced here: 82.3 us
  Pallas kernels  79.2 us (96%)
  local copies, waits for them, and re-layouts  3.13 us (4%)
    pallas_call x1, Pallas kernels, per_device(): pl.pallas_call(functools.partial(kernel, mesh_shape), out_shape=jax.Shape...  79.2 us
    unnamed x1, local copies, waits for them, and re-layouts  3.13 us

profile of v4, /device:TPU:0, one launch (start us, length us, event | category | flops | bytes accessed | tf_op | source)
XLA Modules:
  0.0 82.3 jit_solution(7662424735215809286)
XLA Ops:
  0.0 79.2 %shard_map.118 = f32[32,64,256]{2,1,0:T(8,128)} custom-call(bf16[32,64,256]{2,1,0:T(8,128)(2,1)} %bitcast.9, bf16[32,64,256]{2,1,0:T(8,128)(2,1)} %bitcast.10, f32[1,256]{1,0:T(1,128)} %bitcast.14, f32[25,2,256]{2,1,0:T(2,128)} %bitcast.11, f32[2,256]{1,0:T(2,128)} %gains.1, bf16[2,256,512]{2,1,0:T(8,128)(2,1)} %w_in.1, bf16[2,512,256]{2,1,0:T(8,128)(2,1)} %w_out.1, ...), custom_call_target="tpu_custom_call" | custom-call | tf_op jit(solution)/shard_map/pallas_call | solution.py:416
  79.2 3.1 %copy.14 = f32[1,32,64,256]{3,2,1,0:T(8,128)} copy(f32[1,32,64,256]{3,2,1,0:T(8,128)} %bitcast.8) | data formatting | bytes 4194304
